TPU v7x, 32 devices: a whole 2x2x4 slice. The times are simulated.
32 devices in a mesh: seq: 4 (over y, x), win: 8 (over z, core).
Axes of the slice: x: 2, y: 2, z: 4, core: 2. Of those that a mesh axis runs over, the one named last changes fastest.
Arguments:
- inputs: bfloat16 [8, 1536, 1536], P('win', 'seq'), may hold values from -6 to 6
- bin_order: int32 [8, 1536], P('win'), may hold values from 0 to 1535, as said below
- first_gain: bfloat16 [1536], P('seq'), may hold values from 0.5 to 1.5
- first_shift: bfloat16 [1536], P('seq'), may hold values from -1 to 1
- query_weight: bfloat16 [1536, 512], P('seq'), may hold values from -0.15625 to 0.15625
- key_weight: bfloat16 [1536, 512], P('seq'), may hold values from -0.15625 to 0.15625
- value_weight: bfloat16 [1536, 1536], P('seq'), may hold values from -0.15625 to 0.15625
- bias_content: bfloat16 [512], P('seq'), may hold values from -0.75 to 0.75
- bias_position: bfloat16 [512], P('seq'), may hold values from -0.75 to 0.75
- relative_weight: bfloat16 [192, 512], P('seq'), may hold values from -0.875 to 0.875
- out_weight: bfloat16 [1536, 1536], P('seq'), may hold values from -2 to 2
- bias_out: bfloat16 [1536], P('seq'), may hold values from -1 to 1
- second_gain: bfloat16 [1536], P('seq'), may hold values from 0.5 to 1.5
- second_shift: bfloat16 [1536], P('seq'), may hold values from -1 to 1
- inner_weight: bfloat16 [1536, 3072], P('seq'), may hold values from -0.15625 to 0.15625
- bias_inner: bfloat16 [3072], P('seq'), may hold values from -1 to 1
- outer_weight: bfloat16 [3072, 1536], P('seq'), may hold values from -0.109375 to 0.109375
- bias_outer: bfloat16 [1536], P('seq'), may hold values from -1 to 1
- grad_output: bfloat16 [8, 1536, 1536], P('win', 'seq'), may hold values from -6 to 6
Outputs:
- layer_output: bfloat16 [8, 1536, 1536], P('win', 'seq')
- grad_inputs: float32 [8, 1536, 1536], P('win', 'seq')
- grad_first_gain: float32 [1536], P('seq')
- grad_first_shift: float32 [1536], P('seq')
- grad_query_weight: float32 [1536, 512], P('seq')
- grad_key_weight: float32 [1536, 512], P('seq')
- grad_value_weight: float32 [1536, 1536], P('seq')
- grad_bias_content: float32 [512], P('seq')
- grad_bias_position: float32 [512], P('seq')
- grad_relative_weight: float32 [192, 512], P('seq')
- grad_out_weight: float32 [1536, 1536], P('seq')
- grad_bias_out: float32 [1536], P('seq')
- grad_second_gain: float32 [1536], P('seq')
- grad_second_shift: float32 [1536], P('seq')
- grad_inner_weight: float32 [1536, 3072], P('seq')
- grad_bias_inner: float32 [3072], P('seq')
- grad_outer_weight: float32 [3072, 1536], P('seq')
- grad_bias_outer: float32 [1536], P('seq')
Inputs may be any that keep to these rules, and one draw needn't show every extreme that they name: Each row of bin_order is a permutation of the bins of its window: position i takes bin (s + i) mod 1536 or (s + 1535 - i) mod 1536, with the offset s and the reversal chosen for each window.
All inputs are finite; a program needn't handle non-finite values.
Results may differ from a plain program's by a relative error of at most 0.025.
Values may be sent and summed in bfloat16 or wider, within the bound.
No kernel may reach another device: no remote copies, remote signals or barrier semaphores. Data moves between devices by JAX's collectives and lax.ppermute only.
A program may use at most 320 MiB of HBM per device.

v0:
```python
import functools
import math

import jax
import jax.numpy as jnp
import numpy as np
from jax import lax
from jax.experimental import pallas as pl
from jax.experimental.pallas import tpu as pltpu
from jax.sharding import Mesh
from jax.sharding import PartitionSpec as P

HEADS = 8
KEY = 64
VAL = 192
REL = 192
BF16 = jnp.bfloat16
F32 = jnp.float32
VMEM_LIMIT = 56 * 2**20
EXTRA = 32


def matmul(a, b):
    return lax.dot_general(a, b, (((1,), (0,)), ((), ())), preferred_element_type=F32)


def matmul_nt(a, b):
    return lax.dot_general(a, b, (((1,), (1,)), ((), ())), preferred_element_type=F32)


def matmul_tn(a, b):
    return lax.dot_general(a, b, (((0,), (0,)), ((), ())), preferred_element_type=F32)


def head_part(rows, head):
    lanes = lax.broadcasted_iota(jnp.int32, rows.shape, 1)
    inside = (lanes >= head * KEY) & (lanes < (head + 1) * KEY)
    return jnp.where(inside, rows, jnp.zeros_like(rows))


def head_columns(key_width):
    return [slice(k * key_width, (k + 1) * key_width) for k in range(3)]


def attend_kernel(heads, rows, placed, rel, table, mixed, probs):
    length = placed.shape[0]
    key_width = heads * KEY
    content_at, position_at, keys_at = head_columns(key_width)
    first = pl.program_id(0) * rows
    here = pl.ds(pl.multiple_of(first, rows), rows)
    basis = table[:, pl.ds(pl.multiple_of(length - rows - first, rows), length + rows)]
    content, position, keys = placed[here, content_at], placed[here, position_at], placed[:, keys_at]
    parts = []
    for head in range(heads):
        q_basis = matmul_nt(head_part(position, head), rel[...]).astype(BF16)
        grid = matmul(q_basis, basis)
        shifted = pltpu.roll(grid, 0, 1, stride=1, stride_axis=0)[:, rows:]
        scores = matmul_nt(head_part(content, head), keys) + shifted
        top = jnp.max(scores, axis=1, keepdims=True)
        weights = jnp.exp(scores - top)
        total = jnp.sum(weights, axis=1, keepdims=True)
        prob = (weights * (1.0 / total)).astype(BF16)
        probs[head] = prob
        values_at = 3 * key_width + head * VAL
        parts.append(matmul(prob, placed[:, values_at : values_at + VAL]))
    mixed[...] = jnp.concatenate(parts, axis=1).astype(BF16)


def attend(placed, rel, table):
    length = placed.shape[0]
    heads = rel.shape[1] // KEY
    rows = math.gcd(256, length)
    whole = lambda array: pl.BlockSpec(array.shape, lambda i: (0, 0))
    return pl.pallas_call(
        functools.partial(attend_kernel, heads, rows),
        grid=(length // rows,),
        in_specs=[whole(placed), whole(rel), whole(table)],
        out_specs=[
            pl.BlockSpec((rows, heads * VAL), lambda i: (i, 0)),
            pl.BlockSpec((heads, rows, length), lambda i: (0, i, 0)),
        ],
        out_shape=[
            jax.ShapeDtypeStruct((length, heads * VAL), BF16),
            jax.ShapeDtypeStruct((heads, length, length), BF16),
        ],
        compiler_params=pltpu.CompilerParams(vmem_limit_bytes=VMEM_LIMIT),
        cost_estimate=pl.CostEstimate(
            flops=2 * heads * length * length * 1024,
            bytes_accessed=2 * heads * length * length + 8 * length * heads * VAL,
            transcendentals=heads * length * length,
        ),
    )(placed, rel, table)


def attend_back_kernel(heads, head, rows, *refs):
    placed, rel, table, flip, mixed, d_mixed, probs = refs[:7]
    before = refs[7:-5]
    d_heads, d_rel, d_bias, keys_sum, values_sum = refs[-5:]
    length = placed.shape[0]
    key_width = heads * KEY
    content_at, position_at, keys_at = head_columns(key_width)
    step = pl.program_id(0)

    @pl.when(step == 0)
    def _():
        keys_sum[...] = jnp.zeros_like(keys_sum)
        values_sum[...] = jnp.zeros_like(values_sum)
        for k, out in enumerate((d_heads, d_rel, d_bias)):
            out[...] = before[k][...] if before else jnp.zeros_like(out)

    first = pl.multiple_of(step * rows, rows)
    here = pl.ds(first, rows)
    basis = table[:, pl.ds(first, length + rows)]
    content, position, keys = placed[here, content_at], placed[here, position_at], placed[:, keys_at]
    blocks = length // rows
    columns = slice(head * VAL, (head + 1) * VAL)
    values_at = 3 * key_width + head * VAL
    d_part = d_mixed[:, columns]
    delta = jnp.sum(d_part.astype(F32) * mixed[:, columns].astype(F32), axis=1, keepdims=True)
    prob = probs[0]
    values_sum[...] += matmul_tn(d_part, prob)
    d_prob = matmul_nt(d_part, placed[:, values_at : values_at + VAL])
    d_score = (prob.astype(F32) * (d_prob - delta)).astype(BF16)
    keys_sum[...] += matmul_tn(head_part(content, head), d_score)
    d_content = head_part(matmul(d_score, keys), head)
    turned = [
        matmul(d_score[:, (blocks - 1 - b) * rows : (blocks - b) * rows], flip[...])
        for b in range(blocks)
    ]
    turned = jnp.concatenate(turned + [jnp.zeros((rows, rows), F32)], axis=1)
    d_grid = pltpu.roll(turned, 0, 1, stride=1, stride_axis=0).astype(BF16)
    d_basis = matmul_nt(d_grid, basis).astype(BF16)
    d_position = head_part(matmul(d_basis, rel[...]), head)
    d_rel[...] += matmul_tn(d_basis, head_part(position, head))
    d_heads[here, :key_width] += ((d_content + d_position) * KEY ** (-0.5)).astype(BF16)
    d_bias[0:1, :] += jnp.sum(d_content, axis=0, keepdims=True)
    d_bias[1:2, :] += jnp.sum(d_position, axis=0, keepdims=True)

    @pl.when(step == blocks - 1)
    def _():
        d_heads[:, key_width : 2 * key_width] += keys_sum[...].T.astype(BF16)
        values_to = 2 * key_width + head * VAL
        d_heads[:, values_to : values_to + VAL] = values_sum[...].T.astype(BF16)


def attend_back(head, placed, rel, table, mixed, d_mixed, probs, before=()):
    length = placed.shape[0]
    key_width = rel.shape[1]
    heads = key_width // KEY
    val_width = heads * VAL
    rows = math.gcd(256, length)
    at = jnp.arange(rows)
    flip = (at[:, None] + at[None, :] == rows - 1).astype(BF16)
    block = lambda width: pl.BlockSpec((rows, width), lambda i: (i, 0))
    outs = [
        shape((length, 2 * key_width + val_width), BF16),
        shape((REL, key_width), F32),
        shape((8, key_width), F32),
    ]
    return pl.pallas_call(
        functools.partial(attend_back_kernel, heads, head, rows),
        grid=(length // rows,),
        in_specs=[
            whole_spec(placed),
            whole_spec(rel),
            whole_spec(table),
            whole_spec(flip),
            block(val_width),
            block(val_width),
            pl.BlockSpec((1, rows, length), lambda i: (head, i, 0)),
        ]
        + [whole_spec(array) for array in before],
        out_specs=[whole_spec(out) for out in outs],
        out_shape=outs,
        scratch_shapes=[
            pltpu.VMEM((key_width, length), F32),
            pltpu.VMEM((VAL, length), F32),
        ],
        compiler_params=pltpu.CompilerParams(vmem_limit_bytes=VMEM_LIMIT),
        cost_estimate=pl.CostEstimate(
            flops=2 * length * length * 1536,
            bytes_accessed=2 * length * length + 16 * length * val_width,
            transcendentals=0,
        ),
    )(placed, rel, table, flip, mixed, d_mixed, probs, *before)


def norm_back(unit, scale, gain, grad):
    scaled = grad * gain
    mean_one = jnp.mean(scaled, axis=-1, keepdims=True)
    mean_two = jnp.mean(scaled * unit, axis=-1, keepdims=True)
    return (scaled - mean_one - unit * mean_two) * scale


def whole_spec(array):
    zeros = (0,) * len(array.shape)
    return pl.BlockSpec(array.shape, lambda *_: zeros)


def scalar_spec():
    return pl.BlockSpec(memory_space=pltpu.SMEM)


def params(**more):
    return pltpu.CompilerParams(vmem_limit_bytes=VMEM_LIMIT, **more)


def shape(dims, dtype):
    return jax.ShapeDtypeStruct(tuple(dims), dtype)


def basis_constants(window_len):
    features = REL // 6
    f = np.arange(features, dtype=np.float64)
    half_life = 2.0 ** (3.0 + f * (math.log2(window_len) - 3.0) / (features - 1))
    spread = window_len / (2.0 * features)
    first = window_len / features
    centres = first + f * (window_len - first) / (features - 1)
    concentration = (centres / spread) ** 2
    rate = centres / spread**2
    offset = concentration * np.log(rate) - np.array([math.lgamma(c) for c in concentration])
    columns = [math.log(2.0) / half_life, 2.0 ** (f + 1) - 1.0, concentration - 1.0, rate, offset]
    columns += [np.zeros(features)] * 3
    return np.stack(columns, axis=1).astype(np.float32)


def table_kernel(length, constants, forth, back):
    features = REL // 6
    decay, inside_below, power, rate, offset = [constants[:, k : k + 1] for k in range(5)]

    def gamma(distance):
        logged = power * jnp.log(jnp.maximum(distance, 1.0)) - rate * distance + offset
        return jnp.where(distance == 0.0, 0.0, jnp.exp(logged)) + 1e-08

    every = lax.broadcasted_iota(jnp.int32, (1, length), 1).astype(F32)
    peak = jnp.max(gamma(every), axis=1, keepdims=True)
    lanes = lax.broadcasted_iota(jnp.int32, (1, 2 * length), 1).astype(F32)
    for table, signed in ((forth, lanes - length), (back, length - 1 - lanes)):
        distance = jnp.abs(signed)
        sign = jnp.where(signed > 0, 1.0, jnp.where(signed < 0, -1.0, 0.0))
        parts = (
            jnp.exp(-decay * distance),
            jnp.where(inside_below > distance, 1.0, 0.0),
            gamma(distance) / peak,
        )
        for k, part in enumerate(parts):
            table[k * features : (k + 1) * features, :] = part.astype(BF16)
            table[(3 + k) * features : (4 + k) * features, :] = (sign * part).astype(BF16)


def basis_tables(constants, length):
    out = shape((REL, 2 * length), BF16)
    return pl.pallas_call(
        functools.partial(table_kernel, length),
        out_shape=[out, out],
        compiler_params=params(),
    )(constants)


def norm_of(rows):
    centre = rows - jnp.mean(rows, axis=1, keepdims=True)
    scale = lax.rsqrt(jnp.mean(centre * centre, axis=1, keepdims=True) + 1e-05)
    return centre * scale, scale


def project_kernel(blocks, row_count, *refs):
    parts, (weight, vectors, bias, window, hidden, heads, flat, block) = refs[:blocks], refs[blocks:]
    step = pl.program_id(0)

    @pl.when(step == 0)
    def _():
        for s in range(weight.shape[0]):
            flat[s * row_count : (s + 1) * row_count, :] = weight[s, :row_count, :]

    for k in range(blocks):

        @pl.when(step == k)
        def _():
            block[...] = parts[k][...]

    window[...] = block[...]
    unit, _ = norm_of(block[...].astype(F32))
    normed = (unit * vectors[0:1, :] + vectors[1:2, :]).astype(BF16)
    hidden[...] = normed
    total = matmul(normed, flat[...])
    key_width = bias.shape[1] // 2
    query = total[:, :key_width] * KEY ** (-0.5)
    heads[:, :key_width] = (query + bias[0:1, :key_width]).astype(BF16)
    heads[:, key_width : 2 * key_width] = (query + bias[0:1, key_width:]).astype(BF16)
    heads[:, 2 * key_width :] = total[:, key_width:].astype(BF16)


def project(parts, weight, vectors, bias, row_count):
    blocks = len(parts)
    rows, width = parts[0].shape
    heads_width = weight.shape[2] + bias.shape[1] // 2
    out = lambda w: pl.BlockSpec((rows, w), lambda i: (i, 0))
    return pl.pallas_call(
        functools.partial(project_kernel, blocks, row_count),
        grid=(blocks,),
        in_specs=[whole_spec(a) for a in (*parts, weight, vectors, bias)],
        out_specs=[
            out(width),
            out(width),
            out(heads_width),
            pl.BlockSpec((width, weight.shape[2]), lambda i: (0, 0)),
        ],
        out_shape=[shape((blocks * rows, w), BF16) for w in (width, width, heads_width)]
        + [shape((width, weight.shape[2]), BF16)],
        scratch_shapes=[pltpu.VMEM((rows, width), BF16)],
        compiler_params=params(),
        cost_estimate=pl.CostEstimate(
            flops=2 * blocks * rows * width * heads_width,
            bytes_accessed=8 * blocks * rows * width,
            transcendentals=0,
        ),
    )(*parts, weight, vectors, bias)


def feed_kernel(count, chunk, *refs):
    parts = 2 * (2 * count - 1)
    where, placed, attended_a, attended_b, grad_rows, vectors, inner_bias = refs[:7]
    weights = refs[7 : 7 + parts]
    layer_output, d_mixed, hidden, activated, d_inner, sums, inner_sums = refs[7 + parts : 14 + parts]
    inner_whole, outer_whole, residual, unit, back, outer_sum, sems = refs[14 + parts :]
    here, core = where[0], where[1]
    copies = []
    for k, whole in enumerate((inner_whole, outer_whole)):
        mine = weights[k * (2 * count - 1) : (k + 1) * (2 * count - 1)]
        size = whole.shape[0] // count
        half = size // 2
        moves = [(mine[0], here * size, size)]
        for m in range(1, count):
            start = jnp.bitwise_xor(here, m) * size
            moves.append((mine[2 * m - 1], start + core * half, half))
            moves.append((mine[2 * m], start + (1 - core) * half, half))
        started = []
        for source, start, rows in moves:
            target = whole.at[pl.ds(pl.multiple_of(start, 16), rows), :]
            copy = pltpu.make_async_copy(source, target, sems.at[k, len(started)])
            copy.start()
            started.append(copy)
        copies.append(started)
    rows, width = placed.shape
    half = width // 2
    residual[:, :half] = placed[:, :half] + attended_a[...] + vectors[2:3, :half]
    residual[:, half:] = placed[:, half:] + attended_b[...] + vectors[2:3, half:]
    normed, scale = norm_of(residual[...])
    unit[...] = normed
    hidden[...] = (normed * vectors[3:4, :] + vectors[4:5, :]).astype(BF16)
    for started in copies:
        for copy in started:
            copy.wait()
    ff = outer_whole.shape[0]
    for c in range(ff // chunk):
        at = slice(c * chunk, (c + 1) * chunk)
        inner = matmul(hidden[...], inner_whole[:, at]) + inner_bias[0:1, at]
        below = 0.5 * (1.0 + lax.erf(inner * (0.5**0.5)))
        slope = below + inner * jnp.exp(-0.5 * inner * inner) * (0.5 / math.pi) ** 0.5
        active = (inner * below).astype(BF16)
        activated[:, at] = active
        grad = (matmul_nt(grad_rows[...], outer_whole[at, :]) * slope).astype(BF16)
        d_inner[:, at] = grad
        inner_sums[:, at] = jnp.sum(grad.astype(F32), axis=0, keepdims=True)
        back_term = matmul_nt(grad, inner_whole[:, at])
        outer_term = matmul(active, outer_whole[at, :])
        if c == 0:
            back[...] = back_term
            outer_sum[...] = outer_term
        else:
            back[...] += back_term
            outer_sum[...] += outer_term
    layer_output[...] = (residual[...] + outer_sum[...] + vectors[5:6, :]).astype(BF16)
    grad, normed = back[...], unit[...]
    dy = grad_rows[...].astype(F32)
    scaled = grad * vectors[3:4, :]
    mean_one = jnp.mean(scaled, axis=1, keepdims=True)
    mean_two = jnp.mean(scaled * normed, axis=1, keepdims=True)
    mixed_in = (dy + (scaled - mean_one - normed * mean_two) * scale).astype(BF16)
    d_mixed[...] = mixed_in
    sums[...] = jnp.zeros_like(sums)
    sums[2:3, :] = jnp.sum(mixed_in.astype(F32), axis=0, keepdims=True)
    sums[3:4, :] = jnp.sum(grad * normed, axis=0, keepdims=True)
    sums[4:5, :] = jnp.sum(grad, axis=0, keepdims=True)
    sums[5:6, :] = jnp.sum(dy, axis=0, keepdims=True)


def feed_forward(where, placed, attended, grad_rows, vectors, inner_bias, inner_parts, outer_parts):
    rows, width = placed.shape
    ff = inner_bias.shape[1]
    count = (len(inner_parts) + 1) // 2
    chunk = math.gcd(512, ff)
    weights = (*inner_parts, *outer_parts)
    small = (placed, *attended, grad_rows, vectors, inner_bias)
    outs = [
        shape((rows, width), BF16),
        shape((rows, width), BF16),
        shape((rows, width), BF16),
        shape((rows, ff), BF16),
        shape((rows, ff), BF16),
        shape((8, width), F32),
        shape((1, ff), F32),
    ]
    return pl.pallas_call(
        functools.partial(feed_kernel, count, chunk),
        in_specs=[scalar_spec()]
        + [pl.BlockSpec(memory_space=pltpu.VMEM) for _ in small]
        + [pl.BlockSpec(memory_space=pl.ANY) for _ in weights],
        out_specs=[pl.BlockSpec(memory_space=pltpu.VMEM) for _ in outs],
        out_shape=outs,
        scratch_shapes=[
            pltpu.VMEM((width, ff), BF16),
            pltpu.VMEM((ff, width), BF16),
            pltpu.VMEM((rows, width), F32),
            pltpu.VMEM((rows, width), F32),
            pltpu.VMEM((rows, width), F32),
            pltpu.VMEM((rows, width), F32),
            pltpu.SemaphoreType.DMA((2, 2 * count - 1)),
        ],
        compiler_params=params(),
        cost_estimate=pl.CostEstimate(
            flops=8 * rows * width * ff,
            bytes_accessed=4 * width * ff + 40 * rows * width,
            transcendentals=2 * rows * ff,
        ),
    )(where, *small, *weights)


def columns_at(ref, index, size, scratch):
    if size % 128 == 0:
        return ref[:, pl.ds(pl.multiple_of(index * size, 128), size)]
    for k in range(ref.shape[1] // size):

        @pl.when(index == k)
        def _():
            scratch[...] = ref[:, k * size : (k + 1) * size]

    return scratch[...]


def half_kernel(count, split, away, where, left, right, *refs):
    here, core = where[0], where[1]
    side = 1 - core if away else core
    shard = jnp.bitwise_xor(here, pl.program_id(0))
    if split:
        some = columns_at(left, shard, left.shape[1] // count, refs[-1])
        half = right.shape[1] // 2
        other = right[:, pl.ds(pl.multiple_of(side * half, 128), half)]
    else:
        some = columns_at(left, 2 * shard + side, left.shape[1] // count // 2, refs[-1])
        other = right[...]
    result = matmul_tn(some, other)
    if away:
        refs[0][0] = result.astype(BF16)
        return
    came, outs = refs[0], refs[1:-1]
    result += came[0].astype(F32)
    width = result.shape[1] // 2
    for m in range(count):

        @pl.when(pl.program_id(0) == m)
        def _():
            outs[2 * m][...] = result[:, :width].astype(BF16)
            outs[2 * m + 1][...] = result[:, width:].astype(BF16)


def half_gradient(count, split, where, left, right, came=None):
    away = came is None
    rows = left.shape[1] // count // (1 if split else 2)
    width = right.shape[1] // (2 if split else 1)
    block = pl.BlockSpec((1, rows, width), lambda i: (i, 0, 0))
    if away:
        outs, out_specs = shape((count, rows, width), BF16), block
    else:
        outs = [shape((rows, width // 2), BF16) for _ in range(2 * count)]
        out_specs = [whole_spec(out) for out in outs]
    return pl.pallas_call(
        functools.partial(half_kernel, count, split, away),
        grid=(count,),
        in_specs=[scalar_spec(), whole_spec(left), whole_spec(right)] + ([] if away else [block]),
        out_specs=out_specs,
        out_shape=outs,
        scratch_shapes=[pltpu.VMEM((left.shape[0], rows), BF16)],
        compiler_params=params(),
        cost_estimate=pl.CostEstimate(
            flops=2 * left.shape[0] * count * rows * width,
            bytes_accessed=4 * count * rows * width + 4 * left.shape[0] * left.shape[1],
            transcendentals=0,
        ),
    )(where, left, right, *(() if away else (came,)))


def mixed_back_kernel(count, parts_count, *refs):
    where, mixed, weight = refs[:3]
    parts = refs[3 : 3 + parts_count]
    d_attended, out_away, out_kept, out_sum = refs[3 + parts_count :]
    here, core = where[0], where[1]
    rows = parts[0].shape[0]
    for k, part in enumerate(parts):
        start = jnp.bitwise_xor(here, k // 2) * (2 * rows) + (k % 2) * rows
        at = pl.ds(pl.multiple_of(start, 32), rows)
        d_attended[at, :] = matmul_nt(part[...], weight[...]).astype(BF16)
        term = matmul_tn(mixed[at, :], part[...])
        if k == 0:
            out_sum[...] = term
        else:
            out_sum[...] += term
    half = out_kept.shape[0]
    out_kept[...] = out_sum[pl.ds(pl.multiple_of(core * half, 32), half), :]
    out_away[...] = out_sum[pl.ds(pl.multiple_of((1 - core) * half, 32), half), :].astype(BF16)


def mixed_back(count, where, mixed, weight, parts):
    length, val_width = mixed.shape
    width = weight.shape[1]
    vmem = pl.BlockSpec(memory_space=pltpu.VMEM)
    return pl.pallas_call(
        functools.partial(mixed_back_kernel, count, len(parts)),
        in_specs=[scalar_spec()] + [vmem] * (2 + len(parts)),
        out_specs=[vmem] * 3,
        out_shape=[
            shape((length, val_width), BF16),
            shape((val_width // 2, width), BF16),
            shape((val_width // 2, width), F32),
        ],
        scratch_shapes=[pltpu.VMEM((val_width, width), F32)],
        compiler_params=params(),
        cost_estimate=pl.CostEstimate(
            flops=4 * length * val_width * width,
            bytes_accessed=2 * length * (width + 2 * val_width),
            transcendentals=0,
        ),
    )(where, mixed, weight, *parts)


def rows_back_kernel(count, where, order, d_heads, window, weight, d_along, *refs):
    d_normed, first_sums = refs[:-1], refs[-1]
    here = where[0]
    step = pl.program_id(0)
    rows, width = window.shape
    length = order.shape[1]
    bins = lax.broadcasted_iota(jnp.int32, (rows, length), 0) + jnp.bitwise_xor(here, step) * rows
    picks = jnp.where(order[0:1, :] == bins, 1.0, 0.0).astype(BF16)
    along = matmul(picks, d_heads[...]).astype(BF16)
    d_along[...] = along
    unit, _ = norm_of(window[...].astype(F32))
    normed = matmul_nt(along, weight[...])

    @pl.when(step == 0)
    def _():
        first_sums[...] = jnp.zeros_like(first_sums)

    first_sums[0:1, :] += jnp.sum(normed * unit, axis=0, keepdims=True)
    first_sums[1:2, :] += jnp.sum(normed, axis=0, keepdims=True)
    half = width // 2
    for m in range(count):

        @pl.when(step == m)
        def _():
            d_normed[2 * m][...] = normed[:, :half].astype(BF16)
            d_normed[2 * m + 1][...] = normed[:, half:].astype(BF16)


def rows_back(count, where, order, d_heads, window, weight):
    length, width = window.shape
    rows = length // count
    heads_width = d_heads.shape[1]
    outs = [shape((length, heads_width), BF16)]
    outs += [shape((rows, width // 2), BF16) for _ in range(2 * count)]
    outs += [shape((8, width), F32)]
    return pl.pallas_call(
        functools.partial(rows_back_kernel, count),
        grid=(count,),
        in_specs=[
            scalar_spec(),
            whole_spec(order),
            whole_spec(d_heads),
            pl.BlockSpec((rows, width), lambda i: (i, 0)),
            whole_spec(weight),
        ],
        out_specs=[pl.BlockSpec((rows, heads_width), lambda i: (i, 0))]
        + [whole_spec(out) for out in outs[1:]],
        out_shape=outs,
        compiler_params=params(),
        cost_estimate=pl.CostEstimate(
            flops=2 * length * heads_width * (length + width),
            bytes_accessed=4 * length * (width + heads_width),
            transcendentals=0,
        ),
    )(where, order, d_heads, window, weight)


def pack_kernel(
    count, where, hidden, d_along, first_sums, sums, inner_sums, d_bias, d_rel, kept, away, grads
):
    here, core = where[0], where[1]
    step = pl.program_id(0)
    row_count = hidden.shape[1] // count
    key_width = d_rel.shape[1]
    terms = matmul_tn(hidden[...], d_along[...])

    @pl.when(step == 0)
    def _():
        for s in range(count):
            grads[s, :row_count, :] = terms[s * row_count : (s + 1) * row_count, :]

    @pl.when(step > 0)
    def _():
        for s in range(count):
            grads[s, :row_count, :] += terms[s * row_count : (s + 1) * row_count, :]

    @pl.when(step == pl.num_programs(0) - 1)
    def _():
        rel_rows = d_rel.shape[0] // count
        for s in range(count):
            at = slice(s * row_count, (s + 1) * row_count)
            grads[s, row_count:, :] = jnp.zeros((EXTRA, grads.shape[2]), F32)
            grads[s, row_count : row_count + 2, :row_count] = first_sums[0:2, at]
            grads[s, row_count + 2 : row_count + 6, :row_count] = sums[2:6, at]
            for j in range(2):
                part = slice((2 * s + j) * row_count, (2 * s + j + 1) * row_count)
                grads[s, row_count + 6 + j : row_count + 7 + j, :row_count] = inner_sums[0:1, part]
            for j in range(-(-rel_rows // EXTRA)):
                some = d_rel[s * rel_rows + j * EXTRA : s * rel_rows + min(rel_rows, (j + 1) * EXTRA), :]
                lane = row_count + j * key_width
                grads[s, row_count : row_count + some.shape[0], lane : lane + key_width] = some
        for s in range(count):

            @pl.when(here == s)
            def _():
                grads[s, row_count + 8 : row_count + 10, :key_width] = d_bias[0:2, :]

        half = kept.shape[1]
        kept[...] = grads[:, pl.ds(pl.multiple_of(core * half, 16), half), :].astype(BF16)
        away[...] = grads[:, pl.ds(pl.multiple_of((1 - core) * half, 16), half), :].astype(BF16)


def pack(count, where, hidden, d_along, *small):
    length, width = hidden.shape
    heads_width = d_along.shape[1]
    rows = math.gcd(768, length)
    packed = (count, width // count + EXTRA, heads_width)
    outs = [shape((count, packed[1] // 2, heads_width), BF16) for _ in range(2)]
    return pl.pallas_call(
        functools.partial(pack_kernel, count),
        grid=(length // rows,),
        in_specs=[
            scalar_spec(),
            pl.BlockSpec((rows, width), lambda i: (i, 0)),
            pl.BlockSpec((rows, heads_width), lambda i: (i, 0)),
        ]
        + [whole_spec(a) for a in small],
        out_specs=[whole_spec(out) for out in outs],
        out_shape=outs,
        scratch_shapes=[pltpu.VMEM(packed, F32)],
        compiler_params=params(),
        cost_estimate=pl.CostEstimate(
            flops=2 * length * heads_width * width,
            bytes_accessed=2 * length * (width + heads_width) + 8 * width * heads_width,
            transcendentals=0,
        ),
    )(where, hidden, d_along, *small)


def swap(array, mask, count):
    return lax.ppermute(array, "seq", [(i, i ^ mask) for i in range(count)])


def bit_orders(count):
    bits = [1 << k for k in range(count.bit_length() - 1)]
    return bits, bits[::-1]


def pin(*arrays):
    return lax.optimization_barrier(arrays)


def returned_kernel(count, where, order, *refs):
    parts, returned = refs[:-1], refs[-1]
    here = where[0]
    rows = parts[0].shape[0]
    bins = lax.broadcasted_iota(jnp.int32, (returned.shape[0], rows), 0)
    bins = bins + here * returned.shape[0]
    for k, part in enumerate(parts):
        shard = jnp.bitwise_xor(here, k // 2)
        picks = jnp.where(order[pl.ds(2 * shard + k % 2, 1), :] == bins, 1.0, 0.0).astype(BF16)
        term = matmul(picks, part[...])
        if k == 0:
            returned[...] = term
        else:
            returned[...] += term


def returned_rows(count, where, order, parts):
    rows, width = parts[0].shape
    vmem = pl.BlockSpec(memory_space=pltpu.VMEM)
    return pl.pallas_call(
        functools.partial(returned_kernel, count),
        in_specs=[scalar_spec()] + [vmem] * (1 + len(parts)),
        out_specs=vmem,
        out_shape=shape((2 * rows, width), F32),
        compiler_params=params(),
        cost_estimate=pl.CostEstimate(
            flops=4 * rows * rows * len(parts) * width,
            bytes_accessed=2 * rows * width * len(parts) + 8 * rows * width,
            transcendentals=0,
        ),
    )(where, order, *parts)


def unpack_kernel(count, row_count, key_width, *refs):
    where, mine, theirs, query, key, value, extra, whole = refs
    half = mine.shape[1]
    core = where[1]
    for c in range(2):

        @pl.when(core == c)
        def _():
            whole[:, c * half : (c + 1) * half, :] = mine[...]
            whole[:, (1 - c) * half : (2 - c) * half, :] = theirs[...]

    for out, at in ((query, 0), (key, key_width), (value, 2 * key_width)):
        size = out.shape[1] // count
        for s in range(count):
            rows = whole[s, :row_count, at : at + size]
            out[:, s * size : (s + 1) * size] = rows.astype(F32)
    extra[...] = whole[:, row_count:, :].astype(F32)


def unpack(where, parts, row_count, key_width, val_width):
    count, half, width = parts[0].shape
    vmem = pl.BlockSpec(memory_space=pltpu.VMEM)
    return pl.pallas_call(
        functools.partial(unpack_kernel, count, row_count, key_width),
        in_specs=[scalar_spec()] + [vmem] * 2,
        out_specs=[vmem] * 4,
        out_shape=[
            shape((row_count, count * key_width), F32),
            shape((row_count, count * key_width), F32),
            shape((row_count, count * val_width), F32),
            shape((count, EXTRA, width), F32),
        ],
        scratch_shapes=[pltpu.VMEM((count, 2 * half, width), BF16)],
        compiler_params=params(),
    )(where, *parts)


class Exchange:
    def __init__(self):
        self.new = {}


def pin_all(exchanges, *arrays):
    keys = [sorted(e.new) for e in exchanges]
    out = pin(*arrays, *[e.new[k] for e, ks in zip(exchanges, keys) for k in ks])
    at = len(arrays)
    for e, ks in zip(exchanges, keys):
        e.new = dict(zip(ks, out[at : at + len(ks)]))
        at += len(ks)
    return out[: len(arrays)]


def pin_some(exchanges, *arrays):
    firsts = [max(e.new) for e in exchanges]
    out = pin(*arrays, *[e.new[k] for e, k in zip(exchanges, firsts)])
    for e, k, block in zip(exchanges, firsts, out[len(arrays) :]):
        e.new[k] = block
    return out[: len(arrays)]


class Gather(Exchange):
    def __init__(self, part, order, count):
        super().__init__()
        self.have, self.order, self.count, self.last = {0: part}, order, count, [0]

    def take(self):
        self.have.update(self.new)
        self.new = {}

    def send(self):
        self.take()
        new = {}
        for m in self.last:
            used = [k for k, bit in enumerate(self.order) if m & bit]
            for bit in self.order[max(used, default=-1) + 1 :]:
                new[m | bit] = swap(self.have[m], bit, self.count)
        self.new, self.last = new, sorted(new)


class Scatter(Exchange):
    def __init__(self, blocks, order, count):
        super().__init__()
        self.have, self.order, self.count, self.step = dict(enumerate(blocks)), order, count, 0

    def take(self):
        if self.new:
            bit = self.order[self.step - 1]
            self.have = {
                m: self.have[m].astype(F32) + self.new[m | bit].astype(F32)
                for m in self.have
                if not m & bit
            }
            self.new = {}

    def send(self):
        self.take()
        bit = self.order[self.step]
        self.new = {
            m: swap(self.have[m].astype(BF16), bit, self.count)
            for m in sorted(self.have, reverse=True)
            if m & bit
        }
        self.step += 1

    def rest(self):
        while self.step < len(self.order):
            self.send()
        self.take()
        return self.have[0]


class CubeSum(Exchange):
    def __init__(self, piece, count):
        super().__init__()
        self.total, self.step = piece, 0
        self.count, self.bits = count, count.bit_length() - 1

    def swap(self, array, bit):
        return lax.ppermute(array, "wz", [(i, i ^ bit) for i in range(self.count)])

    def mine(self, bit):
        return jnp.where(lax.axis_index("wz") & bit, 1, 0)

    def take(self):
        if self.new:
            came, at = self.new[0], self.step - 1
            if at < self.bits:
                half = came.shape[0]
                kept = lax.dynamic_slice_in_dim(self.total, self.mine(1 << at) * half, half, 0)
                self.total = (kept.astype(F32) + came.astype(F32)).astype(BF16)
            else:
                upper = self.mine(1 << (2 * self.bits - 1 - at)) == 1
                self.total = jnp.concatenate(
                    [jnp.where(upper, came, self.total), jnp.where(upper, self.total, came)], axis=0
                )
            self.new = {}

    def send(self):
        self.take()
        if self.step >= 2 * self.bits:
            return
        if self.step < self.bits:
            bit = 1 << self.step
            half = self.total.shape[0] // 2
            away = lax.dynamic_slice_in_dim(self.total, (1 - self.mine(bit)) * half, half, 0)
            self.new = {0: self.swap(away.astype(BF16), bit)}
        else:
            self.new = {0: self.swap(self.total, 1 << (2 * self.bits - 1 - self.step))}
        self.step += 1

    def rest(self):
        while self.step < 2 * self.bits:
            self.send()
        self.take()
        return self.total.astype(BF16)


class OtherCore(Exchange):
    def __init__(self, array):
        super().__init__()
        self.new = {0: other_core(array)}


def split_columns(blocks, count):
    half = blocks[0].shape[1] // 2
    return [
        Scatter([block[:, k * half : (k + 1) * half] for block in blocks], order, count)
        for k, order in enumerate(bit_orders(count))
    ]


def other_core(array):
    return lax.ppermute(array, "core", [(0, 1), (1, 0)])


def shards(
    seq_count,
    wz_count,
    inputs,
    bin_order,
    first_gain,
    first_shift,
    query_weight,
    key_weight,
    value_weight,
    bias_content,
    bias_position,
    relative_weight,
    out_weight,
    bias_out,
    second_gain,
    second_shift,
    inner_weight,
    bias_inner,
    outer_weight,
    bias_outer,
    grad_output,
):
    row_count, width = inputs.shape[1:]
    length = bin_order.shape[1]
    here = lax.axis_index("seq")
    core = lax.axis_index("core")
    where = jnp.stack([here, core]).astype(jnp.int32)
    row_start = here * row_count
    key_width = query_weight.shape[1] // seq_count
    val_width = value_weight.shape[1] // seq_count
    heads_width = 2 * key_width + val_width
    up, down = bit_orders(seq_count)

    others = [jnp.bitwise_xor(here, m) for m in range(seq_count)]
    along = jnp.concatenate(
        [other * row_count + jnp.arange(row_count, dtype=jnp.int32) for other in others]
    )

    def natural(rows):
        parts = rows.reshape(seq_count, row_count, -1)
        parts = [lax.dynamic_index_in_dim(parts, other, 0) for other in others]
        return jnp.concatenate(parts, axis=0).reshape(rows.shape)

    def halves(rows):
        half = rows.shape[0] // 2
        return [Gather(rows[:half], up, seq_count), Gather(rows[half:], down, seq_count)]

    def blocks_of(gathers):
        for g in gathers:
            g.take()
        return [g.have[m] for m in range(seq_count) for g in gathers]

    window_gathers = halves(inputs[0])
    for g in window_gathers:
        g.send()

    def by_head(weight):
        return weight.reshape(weight.shape[0], seq_count, -1)

    vectors = jnp.stack([first_gain, first_shift, bias_out, second_gain, second_shift, bias_outer])
    vectors = jnp.concatenate([vectors, bias_inner.reshape(2, row_count)], axis=0)
    vectors = jnp.pad(vectors, ((0, EXTRA - 8), (0, 0)))
    rel_rows = relative_weight.shape[0]
    rel_blocks = -(-rel_rows // EXTRA)
    rel_part = jnp.pad(by_head(relative_weight), ((0, rel_blocks * EXTRA - rel_rows), (0, 0), (0, 0)))
    rel_part = rel_part.reshape(rel_blocks, EXTRA, seq_count, key_width).transpose(2, 1, 0, 3)
    rel_part = rel_part.reshape(seq_count, EXTRA, -1)
    spare = heads_width - row_count - rel_part.shape[2]
    extra = jnp.concatenate(
        [
            jnp.broadcast_to(vectors[None], (seq_count,) + vectors.shape),
            jnp.pad(rel_part, ((0, 0), (0, 0), (0, spare))),
        ],
        axis=2,
    )
    mine = jnp.concatenate(
        [by_head(query_weight), by_head(key_weight), by_head(value_weight)], axis=2
    ).transpose(1, 0, 2)
    mine = jnp.concatenate([mine, extra], axis=1)
    half = mine.shape[1] // 2
    mine = lax.dynamic_slice_in_dim(mine, core * half, half, 1)

    def own_half(weight):
        half = weight.shape[0] // 2
        return lax.dynamic_slice_in_dim(weight, core * half, half, 0)

    inner_part, outer_part = own_half(inner_weight), own_half(outer_weight)
    mine, inner_part, outer_part = pin_all(window_gathers, mine, inner_part, outer_part)
    for step in range(1, len(up)):
        for g in window_gathers:
            g.send()
    weight_gathers = [
        Gather(inner_part, up, seq_count),
        Gather(outer_part, down, seq_count),
    ]
    for g in weight_gathers:
        g.send()
    mine = lax.all_to_all(mine, "seq", 0, 0, tiled=True)
    (mine,) = pin_all(window_gathers, mine)
    first = core == 0
    theirs = other_core(mine)
    attention_weight = jnp.concatenate(
        [jnp.where(first, mine, theirs), jnp.where(first, theirs, mine)], axis=1
    )
    table, table_back = basis_tables(jnp.asarray(basis_constants(length)), length)
    flat = attention_weight[:, row_count:]
    vectors = flat[:, :8, :row_count].astype(F32)
    inner_bias = vectors[:, 6:8].reshape(1, -1)
    vectors = vectors.transpose(1, 0, 2).reshape(8, width)
    rel = flat[:, :, row_count : row_count + rel_blocks * key_width]
    rel = rel.reshape(seq_count, EXTRA, rel_blocks, key_width).transpose(0, 2, 1, 3)
    rel = rel.reshape(seq_count, rel_blocks * EXTRA, key_width)[:, :rel_rows].reshape(REL, key_width)

    window_blocks = blocks_of(window_gathers)

    order = bin_order[0]
    placing = (order[:, None] == along[None, :]).astype(BF16)
    bias = jnp.concatenate([bias_content, bias_position])[None].astype(F32)
    window, hidden_one, in_bins, weight_whole = project(
        window_blocks, attention_weight, vectors, bias, row_count
    )
    placed_heads = matmul(placing, in_bins).astype(BF16)
    (placed_heads,) = pin_all(weight_gathers, placed_heads)
    for step in range(1, len(up)):
        for g in weight_gathers:
            g.send()
    mixed, probs = attend(placed_heads, rel, table)
    (mixed,) = pin_all(weight_gathers, mixed)
    weight_parts = []
    for g, own in zip(weight_gathers, (inner_weight, outer_weight)):
        g.take()
        parts = [own]
        for m in range(1, seq_count):
            parts += [g.have[m], other_core(g.have[m])]
        weight_parts.append(parts)
    mixed_along = natural(mixed).reshape(seq_count, row_count, val_width)
    attended = [matmul(mixed_along[m], out_weight).astype(BF16) for m in range(seq_count)]
    attended = split_columns(attended, seq_count)
    for g in attended:
        g.send()
    own_order = lax.dynamic_slice_in_dim(order, row_start, row_count, 0)
    placed = matmul((own_order[:, None] == along[None, :]).astype(BF16), window)
    (placed,) = pin_all(attended, placed)
    attended = [g.rest() for g in attended]

    grad_rows = grad_output[0]
    layer_output, d_mixed_in, hidden_two, activated, d_inner, sums, inner_sums = feed_forward(
        where, placed, attended, grad_rows, vectors, inner_bias, *weight_parts
    )

    d_mixed_gathers = halves(d_mixed_in)
    for g in d_mixed_gathers:
        g.send()
    came_inner = other_core(half_gradient(seq_count, True, where, hidden_two, d_inner))
    outer_away = half_gradient(seq_count, False, where, activated, grad_rows)
    (outer_away,) = pin_all(d_mixed_gathers, outer_away)
    for step in range(1, len(up)):
        for g in d_mixed_gathers:
            g.send()
    came_outer = other_core(outer_away)
    kept_inner = half_gradient(seq_count, True, where, hidden_two, d_inner, came_inner)
    kept_outer = half_gradient(seq_count, False, where, activated, grad_rows, came_outer)
    kept = pin_all(d_mixed_gathers, *kept_inner, *kept_outer)
    d_mixed_blocks = blocks_of(d_mixed_gathers)
    count = seq_count
    inner_sums_of, outer_sums_of = [
        [
            Scatter([kept[2 * (k * count + m) + side] for m in range(count)], bits, count)
            for side, bits in enumerate((up, down))
        ]
        for k in range(2)
    ]
    for g in inner_sums_of:
        g.send()

    d_attended, out_away, grad_out_w = mixed_back(
        seq_count, where, mixed, out_weight, d_mixed_blocks
    )
    (d_attended,) = pin_some(inner_sums_of, d_attended)
    out_core = OtherCore(out_away)

    def send_all(exchanges):
        for exchange in exchanges:
            exchange.send()

    def scatter_windows(piece):
        return lax.psum_scatter(piece.astype(BF16), "wz", scatter_dimension=0, tiled=True)

    def gather_windows(piece):
        return lax.all_gather(piece, ("core", "wz"), axis=0, tiled=True)

    def joined_sum(scatters):
        return jnp.concatenate([g.rest().astype(BF16) for g in scatters], axis=1)

    (d_attended,) = pin_all([out_core], d_attended)
    out_sum = scatter_windows(grad_out_w + out_core.new[0].astype(F32))
    back = attend_back(0, placed_heads, rel, table_back, mixed, d_attended, probs)
    *back, out_sum = pin_all(inner_sums_of, *back, out_sum)
    out_sum = gather_windows(out_sum)
    for step in range(1, len(up)):
        send_all(inner_sums_of)
    send_all(outer_sums_of)
    for head in range(1, key_width // KEY):
        back = attend_back(head, placed_heads, rel, table_back, mixed, d_attended, probs, back)
    *back, out_sum = pin_all(inner_sums_of, *back, out_sum)
    d_heads, d_rel, d_bias = back
    inner_sum = scatter_windows(joined_sum(inner_sums_of))
    d_along, *d_normed, first_sums = rows_back(
        seq_count, where, order[None], d_heads, window, weight_whole
    )
    out = pin_all(outer_sums_of, d_along, *d_normed)
    d_along, d_normed = out[0], out[1:]
    for step in range(1, len(up)):
        send_all(outer_sums_of)
    arrived = [
        Scatter([d_normed[2 * m + side] for m in range(count)], bits, count)
        for side, bits in enumerate((up, down))
    ]
    results = pack(
        seq_count, where, hidden_one, d_along, first_sums, sums, inner_sums, d_bias, d_rel
    )
    *results, inner_sum = pin_all(outer_sums_of, *results, inner_sum)
    packed_core = OtherCore(results[1])
    outer_sum = scatter_windows(joined_sum(outer_sums_of))
    inner_sum = gather_windows(inner_sum)
    (packed,) = pin_all([packed_core], results[0])
    packed = (packed.astype(F32) + packed_core.new[0].astype(F32)).astype(BF16)
    packed_shape = packed.shape
    packed = lax.all_to_all(packed, "seq", 0, 0, tiled=True)
    send_all(arrived)
    (packed,) = pin(packed)
    packed_cube = CubeSum(packed.reshape(-1, packed_shape[2]), wz_count)
    packed_cube.send()
    (outer_sum,) = pin_all([packed_cube], outer_sum)
    outer_sum = gather_windows(outer_sum)
    packed_cube.send()
    d_mixed_blocks = pin_all(arrived, *d_mixed_blocks)
    for step in range(1, len(up)):
        send_all(arrived)
    returned = returned_rows(
        seq_count, where, order.reshape(2 * seq_count, row_count // 2), d_mixed_blocks
    )
    (returned,) = pin_all([packed_cube], returned)
    packed_cube.send()
    own_unit, own_scale = norm_of(inputs[0].astype(F32))
    arrived = jnp.concatenate([g.rest() for g in arrived], axis=1)
    grad_inputs = norm_back(own_unit, own_scale, vectors[0:1], arrived) + returned

    def both_halves(pieces, axis):
        half = pieces.shape[0] // 2
        return jnp.concatenate([pieces[:half], pieces[half:]], axis=axis).astype(F32)

    grad_out_w = both_halves(out_sum, 0)
    grad_inputs, grad_out_w = pin_all([packed_cube], grad_inputs, grad_out_w)
    packed_cube.send()
    grad_inner_w = both_halves(inner_sum, 1)
    grad_outer_w = both_halves(outer_sum, 0)
    packed = packed_cube.rest().reshape(packed_shape)
    grad_query_w, grad_key_w, grad_value_w, flat = unpack(
        where, (packed, other_core(packed)), row_count, key_width, val_width
    )
    small = jnp.sum(flat[:, :16, :row_count], axis=0)
    g_gain_one, g_shift_one, g_out_b, g_gain_two, g_shift_two, g_outer_b = small[:6]
    g_inner_b = small[6:8].reshape(-1)
    grad_rel = flat[:, :, row_count : row_count + rel_blocks * key_width]
    grad_rel = grad_rel.reshape(seq_count, EXTRA, rel_blocks, key_width).transpose(2, 1, 0, 3)
    grad_rel = grad_rel.reshape(rel_blocks * EXTRA, -1)[:rel_rows]
    return (
        layer_output[None],
        grad_inputs[None],
        g_gain_one,
        g_shift_one,
        grad_query_w,
        grad_key_w,
        grad_value_w,
        small[8, :key_width],
        small[9, :key_width],
        grad_rel,
        grad_out_w,
        g_out_b,
        g_gain_two,
        g_shift_two,
        grad_inner_w,
        g_inner_b,
        grad_outer_w,
        g_outer_b,
    )


def solution(mesh):
    seq_count = mesh.shape["seq"]
    devices = mesh.devices.reshape(seq_count, -1, 2)
    split_mesh = Mesh(devices, ("seq", "wz", "core"))
    rows = P(("wz", "core"), "seq", None)
    vector = P("seq")
    matrix = P("seq", None)
    weights = (
        vector,
        vector,
        matrix,
        matrix,
        matrix,
        vector,
        vector,
        matrix,
        matrix,
        vector,
        vector,
        vector,
        matrix,
        vector,
        matrix,
        vector,
    )
    return jax.shard_map(
        functools.partial(shards, seq_count, mesh.shape["win"] // 2),
        mesh=split_mesh,
        in_specs=(rows, P(("wz", "core"), None)) + weights + (rows,),
        out_specs=(rows, rows) + weights,
        check_vma=False,
    )
```

profile of v0, /device:TPU:0, one launch (start us, length us, event | category | flops | bytes accessed | tf_op | source)
XLA Modules:
  0.0 557.7 jit_solution(13420911956988241319)
XLA Ops:
  29.2 9.7 %collective-permute-done.2.refs_3_ = bf16[192,1536]{1,0:T(8,128)(2,1)} collective-permute-done((bf16[192,1536]{1,0:T(8,128)(2,1)}, bf16[192,1536]{1,0:T(8,128)(2,1)}, u32[]{:S(2)}, u32[]{:S(2)}) %collective-permute-start.2) | collective-permute-done | bytes 589856 | tf_op jit(solution)/shard_map/ppermute | solution.py:666
  47.6 21.8 %collective-permute-done.4.refs_6_ = bf16[192,1536]{1,0:T(8,128)(2,1)S(1)} collective-permute-done((bf16[192,1536]{1,0:T(8,128)(2,1)}, bf16[192,1536]{1,0:T(8,128)(2,1)S(1)}, u32[]{:S(2)}, u32[]{:S(2)}) %collective-permute-start.4) | collective-permute-done | bytes 589856 | tf_op jit(solution)/shard_map/ppermute | solution.py:666
  78.6 12.4 %shard_map.331 = (bf16[1536,1536]{1,0:T(8,128)(2,1)}, bf16[1536,1536]{1,0:T(8,128)(2,1)}, bf16[1536,768]{1,0:T(8,128)(2,1)}, bf16[1536,640]{1,0:T(8,128)(2,1)}) custom-call(bf16[192,1536]{1,0:T(8,128)(2,1)} %get-tuple-element.357.refs_0_, bf16[192,1536]{1,0:T(8,128)(2,1)} %get-tuple-element.356.refs_1_, bf16[192,1536]{1,0:T(8,128)(2,1)} %collective-permute-done.refs_2_, ...), custom_call_target="tpu_custom_call" | custom-call | flops 3623878656 | bytes 18874368 | tf_op jit(solution)/shard_map/pallas_call | solution.py:298
  91.0 7.0 %fusion.4.placed.refs_0_ = bf16[1536,768]{1,0:T(8,128)(2,1)} fusion(bf16[1536,768]{1,0:T(8,128)(2,1)} %get-tuple-element.187, s32[1536]{0:T(1024)S(1)} %pad_add_fusion, s32[1536]{0:T(1024)S(1)} %reduce.2), kind=kOutput, calls=%fused_computation.4 | convolution fusion | flops 3627417600 | bytes 4730880 | tf_op jit(solution)/shard_map/dot_general | solution.py:24
  98.0 28.0 %collective-permute-done.10.refs_17_ = bf16[384,1536]{1,0:T(8,128)(2,1)} collective-permute-done((bf16[384,1536]{1,0:T(8,128)(2,1)S(1)}, bf16[384,1536]{1,0:T(8,128)(2,1)}, u32[]{:S(2)}, u32[]{:S(2)}) %collective-permute-start.10) | collective-permute-done | bytes 1179680 | tf_op jit(solution)/shard_map/ppermute | solution.py:666
  131.0 21.3 %shard_map.333 = (bf16[1536,384]{1,0:T(8,128)(2,1)}, bf16[2,1536,1536]{2,1,0:T(8,128)(2,1)}) custom-call(bf16[1536,768]{1,0:T(8,128)(2,1)} %fusion.4.placed.refs_0_, bf16[192,128]{1,0:T(8,128)(2,1)} %bitcast.112, bf16[192,3072]{1,0:T(8,128)(2,1)} %get-tuple-element.191.table), custom_call_target="tpu_custom_call" | custom-call | flops 9663676416 | bytes 14155776 | tf_op jit(solution)/shard_map/pallas_call | solution.py:74
  174.2 9.5 %collective-permute-done.15 = bf16[384,768]{1,0:T(8,128)(2,1)} collective-permute-done((bf16[384,768]{1,0:T(8,128)(2,1)}, bf16[384,768]{1,0:T(8,128)(2,1)}, u32[]{:S(2)}, u32[]{:S(2)}) %collective-permute-start.15) | collective-permute-done | bytes 589856 | tf_op jit(solution)/shard_map/ppermute | solution.py:666
  189.5 7.7 %collective-permute-done.17 = bf16[384,768]{1,0:T(8,128)(2,1)S(1)} collective-permute-done((bf16[384,768]{1,0:T(8,128)(2,1)S(1)}, bf16[384,768]{1,0:T(8,128)(2,1)S(1)}, u32[]{:S(2)}, u32[]{:S(2)}) %collective-permute-start.17) | collective-permute-done | bytes 589856 | tf_op jit(solution)/shard_map/ppermute | solution.py:666
  206.2 28.4 %shard_map.334 = (bf16[384,1536]{1,0:T(8,128)(2,1)}, bf16[384,1536]{1,0:T(8,128)(2,1)}, bf16[384,1536]{1,0:T(8,128)(2,1)}, bf16[384,3072]{1,0:T(8,128)(2,1)}, bf...) custom-call(s32[2]{0:T(128)} %pad_add_fusion.1.refs_0_.where, f32[384,1536]{1,0:T(8,128)} %fusion.17.refs_1_, ...), custom_call_target="tpu_custom_call" | custom-call | flops 14495514624 | bytes 42467328 | tf_op jit(solution)/shard_map/pallas_call | solution.py:404
  240.1 6.7 %shard_map.336 = bf16[4,384,1536]{2,1,0:T(8,128)(2,1)} custom-call(s32[2]{0:T(128)} %pad_add_fusion.1.refs_0_.where, bf16[384,1536]{1,0:T(8,128)(2,1)} %get-tuple-element.213.left, bf16[384,3072]{1,0:T(8,128)(2,1)} %get-tuple-element.214.right), custom_call_target="tpu_custom_call" | custom-call | flops 1811939328 | bytes 11796480 | tf_op jit(solution)/shard_map/pallas_call | solution.py:477
  246.8 6.5 %shard_map.335 = bf16[4,384,1536]{2,1,0:T(8,128)(2,1)} custom-call(s32[2]{0:T(128)} %pad_add_fusion.1.refs_0_.where, bf16[384,3072]{1,0:T(8,128)(2,1)} %get-tuple-element.208.left, bf16[384,1536]{1,0:T(8,128)(2,1)} %bitcast.90), custom_call_target="tpu_custom_call" | custom-call | flops 1811939328 | bytes 14155776 | tf_op jit(solution)/shard_map/pallas_call | solution.py:477
  253.7 10.8 %collective-permute-done.27.refs_6_.refs_3_ = bf16[192,1536]{1,0:T(8,128)(2,1)S(1)} collective-permute-done((bf16[192,1536]{1,0:T(8,128)(2,1)S(1)}, bf16[192,1536]{1,0:T(8,128)(2,1)S(1)}, u32[]{:S(2)}, u32[]{:S(2)}) %collective-permute-start.27) | collective-permute-done | bytes 589856 | tf_op jit(solution)/shard_map/ppermute | solution.py:666
  269.2 8.8 %shard_map.337 = (bf16[384,768]{1,0:T(8,128)(2,1)}, bf16[384,768]{1,0:T(8,128)(2,1)}, bf16[384,768]{1,0:T(8,128)(2,1)}, bf16[384,768]{1,0:T(8,128)(2,1)}, bf16[3...) custom-call(s32[2]{0:T(128)} %pad_add_fusion.1.refs_0_.where, ...), custom_call_target="tpu_custom_call" | custom-call | flops 1811939328 | bytes 11796480 | tf_op jit(solution)/shard_map/pallas_call | solution.py:477
  278.1 9.0 %shard_map.338 = (bf16[384,768]{1,0:T(8,128)(2,1)}, bf16[384,768]{1,0:T(8,128)(2,1)}, bf16[384,768]{1,0:T(8,128)(2,1)}, bf16[384,768]{1,0:T(8,128)(2,1)}, bf16[3...) custom-call(s32[2]{0:T(128)} %pad_add_fusion.1.refs_0_.where, ...), custom_call_target="tpu_custom_call" | custom-call | flops 1811939328 | bytes 14155776 | tf_op jit(solution)/shard_map/pallas_call | solution.py:477
  290.7 9.9 %shard_map.339 = (bf16[1536,384]{1,0:T(8,128)(2,1)}, bf16[192,1536]{1,0:T(8,128)(2,1)}, f32[192,1536]{1,0:T(8,128)}) custom-call(s32[2]{0:T(128)} %pad_add_fusion.1.refs_0_.where, bf16[1536,384]{1,0:T(8,128)(2,1)} %get-tuple-element.195.refs_1_.refs_4_, bf16[384,1536]{1,0:T(8,128)(2,1)} %refs_2_.1, bf16[192,1536]{1,0:T(8,128)(2,1)} %copy-done.8, ...), custom_call_target="tpu_custom_call" | custom-call | flops 3623878656 | bytes 7077888 | tf_op jit(solution)/shard_map/pallas_call | solution.py:517
  309.2 16.5 %shard_map.340 = (bf16[1536,640]{1,0:T(8,128)(2,1)}, f32[192,128]{1,0:T(8,128)}, f32[8,128]{1,0:T(8,128)}) custom-call(bf16[1536,768]{1,0:T(8,128)(2,1)} %fusion.4.placed.refs_0_, bf16[192,128]{1,0:T(8,128)(2,1)} %bitcast.113, bf16[192,3072]{1,0:T(8,128)(2,1)} %get-tuple-element.206.refs_2_, bf16[256,256]{1,0:T(8,128)(2,1)} %fusion.35.refs_3_, ...), custom_call_target="tpu_custom_call" | custom-call | flops 7247757312 | bytes 14155776 | tf_op jit(solution)/shard_map/pallas_call | solution.py:160
  332.3 18.3 %shard_map.341 = (bf16[1536,640]{1,0:T(8,128)(2,1)}, f32[192,128]{1,0:T(8,128)}, f32[8,128]{1,0:T(8,128)}) custom-call(bf16[1536,768]{1,0:T(8,128)(2,1)} %fusion.4.placed.refs_0_, bf16[192,128]{1,0:T(8,128)(2,1)} %bitcast.114, bf16[192,3072]{1,0:T(8,128)(2,1)} %get-tuple-element.206.refs_2_, bf16[256,256]{1,0:T(8,128)(2,1)} %fusion.35.refs_3_, ...), custom_call_target="tpu_custom_call" | custom-call | flops 7247757312 | bytes 14155776 | tf_op jit(solution)/shard_map/pallas_call | solution.py:160
  358.1 18.6 %shard_map.342 = (bf16[1536,640]{1,0:T(8,128)(2,1)}, bf16[384,768]{1,0:T(8,128)(2,1)}, bf16[384,768]{1,0:T(8,128)(2,1)}, bf16[384,768]{1,0:T(8,128)(2,1)}, bf16[...) custom-call(s32[2]{0:T(128)} %pad_add_fusion.1.refs_0_.where, ...), custom_call_target="tpu_custom_call" | custom-call | flops 6039797760 | bytes 13369344 | tf_op jit(solution)/shard_map/pallas_call | solution.py:571
  387.0 8.4 %shard_map.344 = (bf16[4,208,640]{2,1,0:T(8,128)(2,1)}, bf16[4,208,640]{2,1,0:T(8,128)(2,1)}) custom-call(s32[2]{0:T(128)} %pad_add_fusion.1.refs_0_.where, bf16[1536,1536]{1,0:T(8,128)(2,1)} %get-tuple-element.296.hidden, bf16[1536,640]{1,0:T(8,128)(2,1)} %get-tuple-element.297.d_along, f32[8,1536]{1,0:T(8,128)} %get-tuple-element.298.first_sums, ...), custom_call_target="tpu_custom_call" | custom-call | flops 3019898880 | bytes 14548992 | tf_op jit(solution)/shard_map/pallas_call | solution.py:644
  407.9 11.8 %collective-permute-done.44 = bf16[384,768]{1,0:T(8,128)(2,1)S(1)} collective-permute-done((bf16[384,768]{1,0:T(8,128)(2,1)}, bf16[384,768]{1,0:T(8,128)(2,1)S(1)}, u32[]{:S(2)}, u32[]{:S(2)}) %collective-permute-start.44) | collective-permute-done | bytes 589856 | tf_op jit(solution)/shard_map/ppermute | solution.py:666
  419.7 12.2 %collective-permute-done.45 = bf16[384,768]{1,0:T(8,128)(2,1)S(1)} collective-permute-done((bf16[384,768]{1,0:T(8,128)(2,1)}, bf16[384,768]{1,0:T(8,128)(2,1)S(1)}, u32[]{:S(2)}, u32[]{:S(2)}) %collective-permute-start.45) | collective-permute-done | bytes 589856 | tf_op jit(solution)/shard_map/ppermute | solution.py:666
  479.8 10.4 %collective-permute-done.54 = bf16[208,640]{1,0:T(8,128)(2,1)} collective-permute-done((bf16[208,640]{1,0:T(8,128)(2,1)}, bf16[208,640]{1,0:T(8,128)(2,1)}, u32[]{:S(2)}, u32[]{:S(2)}) %collective-permute-start.54) | collective-permute-done | bytes 266272 | tf_op jit(solution)/shard_map/ppermute | solution.py:829
  495.3 22.8 %collective-permute-done.55 = bf16[208,640]{1,0:T(8,128)(2,1)S(1)} collective-permute-done((bf16[208,640]{1,0:T(8,128)(2,1)S(1)}, bf16[208,640]{1,0:T(8,128)(2,1)S(1)}, u32[]{:S(2)}, u32[]{:S(2)}) %collective-permute-start.55) | collective-permute-done | bytes 266272 | tf_op jit(solution)/shard_map/ppermute | solution.py:829
  518.3 13.2 %collective-permute-done.56 = bf16[416,640]{1,0:T(8,128)(2,1)S(1)} collective-permute-done((bf16[416,640]{1,0:T(8,128)(2,1)S(1)}, bf16[416,640]{1,0:T(8,128)(2,1)S(1)}, u32[]{:S(2)}, u32[]{:S(2)}) %collective-permute-start.56) | collective-permute-done | bytes 532512 | tf_op jit(solution)/shard_map/ppermute | solution.py:829
  (360 shorter events, 212.5 us)
Async XLA Ops:
  14.7 25.7 %collective-permute-start.3 = (bf16[192,1536]{1,0:T(8,128)(2,1)}, bf16[192,1536]{1,0:T(8,128)(2,1)}, u32[]{:S(2)}, u32[]{:S(2)}) collective-permute-start(bf16[192,1536]{1,0:T(8,128)(2,1)} %get-tuple-element.356.refs_1_), channel_id=1, source_target_pairs={{0,16},{8,24},{16,0},{24,8},{1,17},{9,25},{17,1},{25,9},{2,18},{10... | collective-permute-start | bytes 1769480 | tf_op jit(solution)/shard_map/ppermute | solution.py:666
  40.4 29.8 %all-to-all-start = ((bf16[4,208,640]{2,1,0:T(8,128)(2,1)}), bf16[4,208,640]{2,1,0:T(8,128)(2,1)S(1)}, u32[]{:S(2)}, u32[]{:S(2)}) async-start(bf16[4,208,640]{2,1,0:T(8,128)(2,1)} %fusion.22), calls=%async_computation | async-start | bytes 2129920 | tf_op jit(solution)/shard_map/all_to_all | solution.py:984
  43.9 284.9 %reduce-scatter.4.cloned.1.call-start = ((), (), s32[]{:S(2)}) async-start(), calls=%async_computation.5 | async-start | bytes 737280 | tf_op jit(solution)/shard_map/reduce_scatter | solution.py:1073
  70.9 55.2 %collective-permute-start.7 = (bf16[192,3072]{1,0:T(8,128)(2,1)}, bf16[192,3072]{1,0:T(8,128)(2,1)}, u32[]{:S(2)}, u32[]{:S(2)}) collective-permute-start(bf16[192,3072]{1,0:T(8,128)(2,1)} %constant_dynamic-slice_fusion.4), channel_id=1, source_target_pairs={{0,8},{8,0},{16,24},{24,16},{1,9},{9,1},{17,25},{25,17},{2,10},{10... | collective-permute-start | bytes 3538952 | tf_op jit(solution)/shard_map/ppermute | solution.py:666
  72.4 53.7 %collective-permute-start.8 = (bf16[192,3072]{1,0:T(8,128)(2,1)}, bf16[192,3072]{1,0:T(8,128)(2,1)}, u32[]{:S(2)}, u32[]{:S(2)}) collective-permute-start(bf16[192,3072]{1,0:T(8,128)(2,1)} %constant_dynamic-slice_fusion.4), channel_id=1, source_target_pairs={{0,16},{8,24},{16,0},{24,8},{1,17},{9,25},{17,1},{25,9},{2,18},{10... | collective-permute-start | bytes 3538952 | tf_op jit(solution)/shard_map/ppermute | solution.py:666
  73.0 53.1 %collective-permute-start.10 = (bf16[384,1536]{1,0:T(8,128)(2,1)S(1)}, bf16[384,1536]{1,0:T(8,128)(2,1)}, u32[]{:S(2)}, u32[]{:S(2)}) collective-permute-start(bf16[384,1536]{1,0:T(8,128)(2,1)S(1)} %copy-done.11), channel_id=1, source_target_pairs={{0,16},{8,24},{16,0},{24,8},{1,17},{9,25},{17,1},{25,9},{2,18},{10... | collective-permute-start | bytes 3538952 | tf_op jit(solution)/shard_map/ppermute | solution.py:666
  74.5 51.6 %collective-permute-start.9 = (bf16[384,1536]{1,0:T(8,128)(2,1)S(1)}, bf16[384,1536]{1,0:T(8,128)(2,1)}, u32[]{:S(2)}, u32[]{:S(2)}) collective-permute-start(bf16[384,1536]{1,0:T(8,128)(2,1)S(1)} %copy-done.11), channel_id=1, source_target_pairs={{0,8},{8,0},{16,24},{24,16},{1,9},{9,1},{17,25},{25,17},{2,10},{10... | collective-permute-start | bytes 3538952 | tf_op jit(solution)/shard_map/ppermute | solution.py:666
  126.1 27.6 %collective-permute-start.11 = (bf16[192,3072]{1,0:T(8,128)(2,1)}, bf16[192,3072]{1,0:T(8,128)(2,1)}, u32[]{:S(2)}, u32[]{:S(2)}) collective-permute-start(bf16[192,3072]{1,0:T(8,128)(2,1)} %collective-permute-done.7.refs_8_), channel_id=1, source_target_pairs={{0,16},{8,24},{16,0},{24,8},{1,17},{9,25},{17,1},{25,9},{2,18},{10... | collective-permute-start | bytes 3538952 | tf_op jit(solution)/shard_map/ppermute | solution.py:666
  126.7 27.3 %collective-permute-start.12 = (bf16[384,1536]{1,0:T(8,128)(2,1)}, bf16[384,1536]{1,0:T(8,128)(2,1)}, u32[]{:S(2)}, u32[]{:S(2)}) collective-permute-start(bf16[384,1536]{1,0:T(8,128)(2,1)} %collective-permute-done.10.refs_17_), channel_id=1, source_target_pairs={{0,8},{8,0},{16,24},{24,16},{1,9},{9,1},{17,25},{25,17},{2,10},{10... | collective-permute-start | bytes 3538952 | tf_op jit(solution)/shard_map/ppermute | solution.py:666
  238.1 26.3 %collective-permute-start.27 = (bf16[192,1536]{1,0:T(8,128)(2,1)S(1)}, bf16[192,1536]{1,0:T(8,128)(2,1)S(1)}, u32[]{:S(2)}, u32[]{:S(2)}) collective-permute-start(bf16[192,1536]{1,0:T(8,128)(2,1)S(1)} %get-tuple-element.289.refs_4_.refs_1_), channel_id=1, source_target_pairs={{0,8},{8,0},{16,24},{24,16},{1,9},{9,1},{17,25},{25,17},{2,10},{10... | collective-permute-start | bytes 1769480 | tf_op jit(solution)/shard_map/ppermute | solution.py:666
  239.0 26.6 %collective-permute-start.28 = (bf16[192,1536]{1,0:T(8,128)(2,1)S(1)}, bf16[192,1536]{1,0:T(8,128)(2,1)S(1)}, u32[]{:S(2)}, u32[]{:S(2)}) collective-permute-start(bf16[192,1536]{1,0:T(8,128)(2,1)S(1)} %get-tuple-element.289.refs_4_.refs_1_), channel_id=1, source_target_pairs={{0,16},{8,24},{16,0},{24,8},{1,17},{9,25},{17,1},{25,9},{2,18},{10... | collective-permute-start | bytes 1769480 | tf_op jit(solution)/shard_map/ppermute | solution.py:666
  306.4 45.0 %all-gather.4.cloned.1.call-start = ((), (), s32[]{:S(2)}) async-start(), calls=%async_computation.6 | async-start | bytes 1327104 | tf_op jit(solution)/shard_map/all_gather | solution.py:1076
  328.9 70.5 %reduce-scatter.6.cloned.1.call-start = ((), (), s32[]{:S(2)}) async-start(), calls=%async_computation.7 | async-start | bytes 1474560 | tf_op jit(solution)/shard_map/reduce_scatter | solution.py:1073
  353.9 115.2 %reduce-scatter.8.cloned.1.call-start = ((), (), s32[]{:S(2)}) async-start(), calls=%async_computation.8 | async-start | bytes 1474560 | tf_op jit(solution)/shard_map/reduce_scatter | solution.py:1073
  355.5 26.6 %collective-permute-start.41 = (bf16[384,768]{1,0:T(8,128)(2,1)S(1)}, bf16[384,768]{1,0:T(8,128)(2,1)S(1)}, u32[]{:S(2)}, u32[]{:S(2)}) collective-permute-start(bf16[384,768]{1,0:T(8,128)(2,1)S(1)} %copy-done.57), channel_id=1, source_target_pairs={{0,8},{8,0},{16,24},{24,16},{1,9},{9,1},{17,25},{25,17},{2,10},{10... | collective-permute-start | bytes 1769480 | tf_op jit(solution)/shard_map/ppermute | solution.py:666
  356.1 26.1 %collective-permute-start.42 = (bf16[384,768]{1,0:T(8,128)(2,1)S(1)}, bf16[384,768]{1,0:T(8,128)(2,1)S(1)}, u32[]{:S(2)}, u32[]{:S(2)}) collective-permute-start(bf16[384,768]{1,0:T(8,128)(2,1)S(1)} %copy-done.56), channel_id=1, source_target_pairs={{0,16},{8,24},{16,0},{24,8},{1,17},{9,25},{17,1},{25,9},{2,18},{10... | collective-permute-start | bytes 1769480 | tf_op jit(solution)/shard_map/ppermute | solution.py:666
  357.6 26.1 %collective-permute-start.43 = (bf16[384,768]{1,0:T(8,128)(2,1)S(1)}, bf16[384,768]{1,0:T(8,128)(2,1)S(1)}, u32[]{:S(2)}, u32[]{:S(2)}) collective-permute-start(bf16[384,768]{1,0:T(8,128)(2,1)S(1)} %copy-done.55), channel_id=1, source_target_pairs={{0,16},{8,24},{16,0},{24,8},{1,17},{9,25},{17,1},{25,9},{2,18},{10... | collective-permute-start | bytes 1769480 | tf_op jit(solution)/shard_map/ppermute | solution.py:666
  401.8 130.2 %all-gather.6.cloned.1.call-start = ((), (), s32[]{:S(2)}) async-start(), calls=%async_computation.9 | async-start | bytes 2654208 | tf_op jit(solution)/shard_map/all_gather | solution.py:1076
  403.1 32.7 %collective-permute-start.52 = (bf16[4,208,640]{2,1,0:T(8,128)(2,1)S(1)}, bf16[4,208,640]{2,1,0:T(8,128)(2,1)S(1)}, u32[]{:S(2)}, u32[]{:S(2)}) collective-permute-start(bf16[4,208,640]{2,1,0:T(8,128)(2,1)S(1)} %copy-done.54), channel_id=1, source_target_pairs={{0,1},{1,0},{2,3},{3,2},{4,5},{5,4},{6,7},{7,6},{8,9},{9,8},{10,11... | collective-permute-start | bytes 3194888 | tf_op jit(solution)/shard_map/ppermute | solution.py:883
  404.1 27.9 %collective-permute-start.45 = (bf16[384,768]{1,0:T(8,128)(2,1)}, bf16[384,768]{1,0:T(8,128)(2,1)S(1)}, u32[]{:S(2)}, u32[]{:S(2)}) collective-permute-start(bf16[384,768]{1,0:T(8,128)(2,1)} %get-tuple-element.278), channel_id=1, source_target_pairs={{0,8},{8,0},{16,24},{24,16},{1,9},{9,1},{17,25},{25,17},{2,10},{10... | collective-permute-start | bytes 1769480 | tf_op jit(solution)/shard_map/ppermute | solution.py:666
  405.4 26.5 %collective-permute-start.46 = (bf16[384,768]{1,0:T(8,128)(2,1)S(1)}, bf16[384,768]{1,0:T(8,128)(2,1)S(1)}, u32[]{:S(2)}, u32[]{:S(2)}) collective-permute-start(bf16[384,768]{1,0:T(8,128)(2,1)S(1)} %copy-done.60), channel_id=1, source_target_pairs={{0,16},{8,24},{16,0},{24,8},{1,17},{9,25},{17,1},{25,9},{2,18},{10... | collective-permute-start | bytes 1769480 | tf_op jit(solution)/shard_map/ppermute | solution.py:666
  406.9 26.3 %collective-permute-start.47 = (bf16[384,768]{1,0:T(8,128)(2,1)S(1)}, bf16[384,768]{1,0:T(8,128)(2,1)S(1)}, u32[]{:S(2)}, u32[]{:S(2)}) collective-permute-start(bf16[384,768]{1,0:T(8,128)(2,1)S(1)} %copy-done.59), channel_id=1, source_target_pairs={{0,16},{8,24},{16,0},{24,8},{1,17},{9,25},{17,1},{25,9},{2,18},{10... | collective-permute-start | bytes 1769480 | tf_op jit(solution)/shard_map/ppermute | solution.py:666
  440.7 105.4 %all-gather.8.cloned.1.call-start = ((), (), s32[]{:S(2)}) async-start(), calls=%async_computation.10 | async-start | bytes 2654208 | tf_op jit(solution)/shard_map/all_gather | solution.py:1076
  491.3 26.7 %collective-permute-start.55 = (bf16[208,640]{1,0:T(8,128)(2,1)S(1)}, bf16[208,640]{1,0:T(8,128)(2,1)S(1)}, u32[]{:S(2)}, u32[]{:S(2)}) collective-permute-start(bf16[208,640]{1,0:T(8,128)(2,1)S(1)} %add_convert_fusion.15), channel_id=1, source_target_pairs={{0,4},{2,6},{4,0},{6,2},{1,5},{3,7},{5,1},{7,3},{8,12},{10,14},{12... | collective-permute-start | bytes 798728 | tf_op jit(solution)/shard_map/ppermute | solution.py:829
  (106 other events, 1393.4 us)
Sparse Core Ops, SparseCore 0:
  306.6 22.2 reduce-scatter.3
  330.4 21.0 all-gather.3
  354.4 28.9 reduce-scatter.5
  401.9 28.1 reduce-scatter.7
  431.6 30.3 all-gather.5
  478.6 42.2 all-gather.7
where the time goes:
time: 562 us; the launch traced here: 558 us
  waiting for transfers between devices  209 us (37%)
  Pallas kernels  178 us (32%)
  starting transfers between devices  60.8 us (11%)
  other arithmetic  44.3 us (8%)
  local copies, waits for them, and re-layouts  32.3 us (6%)
  matrix products  17.8 us (3%)
  between operations  15.4 us (3%)
    ppermute x42, waiting for transfers between devices, swap(): return lax.ppermute(array, 'seq', [(i, i ^ mask) for i in range(count)])  152 us
    ppermute x4, waiting for transfers between devices, swap(): return lax.ppermute(array, 'wz', [(i, i ^ bit) for i in range(self.count)])  50.9 us
    ppermute x42, starting transfers between devices, swap(): return lax.ppermute(array, 'seq', [(i, i ^ mask) for i in range(count)])  48.7 us
    pallas_call x2, Pallas kernels, attend_back(): pl.pallas_call(functools.partial(attend_back_kernel, heads, head, rows),...  34.8 us
    pallas_call x4, Pallas kernels, half_gradient(): pl.pallas_call(functools.partial(half_kernel, count, split, away), grid=(...  31 us
    pallas_call x1, Pallas kernels, feed_forward(): pl.pallas_call(functools.partial(feed_kernel, count, chunk), in_specs=[sc...  28.4 us
    pallas_call x1, Pallas kernels, attend(): pl.pallas_call(functools.partial(attend_kernel, heads, rows), grid=(lengt...  21.3 us
    pallas_call x1, Pallas kernels, rows_back(): pl.pallas_call(functools.partial(rows_back_kernel, count), grid=(count,),...  18.6 us
  transfers between devices with their start and end apart: 66, of which 34 were waited for; matrix products, arithmetic and copies ran while one was open for 12% of the time, Pallas kernels for 27%

commit v1 on v0

--- a/solution.py
+++ b/solution.py
@@ -760,6 +760,10 @@
     return out[: len(arrays)]
 
 
+def take_after(exchanges, array):
+    pin_all(exchanges, array)
+
+
 def pin_some(exchanges, *arrays):
     firsts = [max(e.new) for e in exchanges]
     out = pin(*arrays, *[e.new[k] for e, k in zip(exchanges, firsts)])
@@ -1006,12 +1010,11 @@
         window_blocks, attention_weight, vectors, bias, row_count
     )
     placed_heads = matmul(placing, in_bins).astype(BF16)
-    (placed_heads,) = pin_all(weight_gathers, placed_heads)
+    mixed, probs = attend(placed_heads, rel, table)
+    (mixed,) = pin_all(weight_gathers, mixed)
     for step in range(1, len(up)):
         for g in weight_gathers:
             g.send()
-    mixed, probs = attend(placed_heads, rel, table)
-    (mixed,) = pin_all(weight_gathers, mixed)
     weight_parts = []
     for g, own in zip(weight_gathers, (inner_weight, outer_weight)):
         g.take()
@@ -1039,12 +1042,12 @@
         g.send()
     came_inner = other_core(half_gradient(seq_count, True, where, hidden_two, d_inner))
     outer_away = half_gradient(seq_count, False, where, activated, grad_rows)
-    (outer_away,) = pin_all(d_mixed_gathers, outer_away)
+    came_outer = other_core(outer_away)
+    kept_inner = half_gradient(seq_count, True, where, hidden_two, d_inner, came_inner)
+    kept_inner = pin_all(d_mixed_gathers, *kept_inner)
     for step in range(1, len(up)):
         for g in d_mixed_gathers:
             g.send()
-    came_outer = other_core(outer_away)
-    kept_inner = half_gradient(seq_count, True, where, hidden_two, d_inner, came_inner)
     kept_outer = half_gradient(seq_count, False, where, activated, grad_rows, came_outer)
     kept = pin_all(d_mixed_gathers, *kept_inner, *kept_outer)
     d_mixed_blocks = blocks_of(d_mixed_gathers)
@@ -1114,7 +1117,7 @@
     packed_shape = packed.shape
     packed = lax.all_to_all(packed, "seq", 0, 0, tiled=True)
     send_all(arrived)
-    (packed,) = pin(packed)
+    take_after(arrived, packed)
     packed_cube = CubeSum(packed.reshape(-1, packed_shape[2]), wz_count)
     packed_cube.send()
     (outer_sum,) = pin_all([packed_cube], outer_sum)

time: 562 us -> 558 us (level)
    ppermute x4, waiting for transfers between devices: 50.9 us -> 43.5 us  [swap(): return lax.ppermute(array, 'wz', [(i, i ^ bit) for i in range(self.count)])]
  transfers between devices with their start and end apart: 66 -> 66, of which waited for: 34 -> 36; matrix products, arithmetic and copies ran while one was open for 12% -> 12% of each run, Pallas kernels for 27% -> 26%
where the time goes in v1:
time: 558 us; the launch traced here: 548 us
  waiting for transfers between devices  207 us (37%)
  Pallas kernels  178 us (32%)
  starting transfers between devices  60 us (11%)
  other arithmetic  42.2 us (8%)
  local copies, waits for them, and re-layouts  27.5 us (5%)
  matrix products  17.8 us (3%)
  between operations  15.5 us (3%)
    ppermute x42, waiting for transfers between devices, swap(): return lax.ppermute(array, 'seq', [(i, i ^ mask) for i in range(count)])  147 us
    ppermute x42, starting transfers between devices, swap(): return lax.ppermute(array, 'seq', [(i, i ^ mask) for i in range(count)])  47 us
    ppermute x4, waiting for transfers between devices, swap(): return lax.ppermute(array, 'wz', [(i, i ^ bit) for i in range(self.count)])  43.5 us
    pallas_call x2, Pallas kernels, attend_back(): pl.pallas_call(functools.partial(attend_back_kernel, heads, head, rows),...  34.8 us
    pallas_call x4, Pallas kernels, half_gradient(): pl.pallas_call(functools.partial(half_kernel, count, split, away), grid=(...  30.9 us
    pallas_call x1, Pallas kernels, feed_forward(): pl.pallas_call(functools.partial(feed_kernel, count, chunk), in_specs=[sc...  28.3 us
    pallas_call x1, Pallas kernels, attend(): pl.pallas_call(functools.partial(attend_kernel, heads, rows), grid=(lengt...  21.3 us
    pallas_call x1, Pallas kernels, rows_back(): pl.pallas_call(functools.partial(rows_back_kernel, count), grid=(count,),...  18.6 us
  transfers between devices with their start and end apart: 66, of which 36 were waited for; matrix products, arithmetic and copies ran while one was open for 12% of the time, Pallas kernels for 26%

profile of v1, /device:TPU:0, one launch (start us, length us, event | category | flops | bytes accessed | tf_op | source)
XLA Modules:
  0.0 548.3 jit_solution(3601966987068679126)
XLA Ops:
  29.2 9.7 %collective-permute-done.2.refs_3_ = bf16[192,1536]{1,0:T(8,128)(2,1)} collective-permute-done((bf16[192,1536]{1,0:T(8,128)(2,1)}, bf16[192,1536]{1,0:T(8,128)(2,1)}, u32[]{:S(2)}, u32[]{:S(2)}) %collective-permute-start.2) | collective-permute-done | bytes 589856 | tf_op jit(solution)/shard_map/ppermute | solution.py:666
  47.4 22.0 %collective-permute-done.4.refs_6_ = bf16[192,1536]{1,0:T(8,128)(2,1)S(1)} collective-permute-done((bf16[192,1536]{1,0:T(8,128)(2,1)}, bf16[192,1536]{1,0:T(8,128)(2,1)S(1)}, u32[]{:S(2)}, u32[]{:S(2)}) %collective-permute-start.4) | collective-permute-done | bytes 589856 | tf_op jit(solution)/shard_map/ppermute | solution.py:666
  81.4 12.5 %shard_map.331 = (bf16[1536,1536]{1,0:T(8,128)(2,1)}, bf16[1536,1536]{1,0:T(8,128)(2,1)}, bf16[1536,768]{1,0:T(8,128)(2,1)}, bf16[1536,640]{1,0:T(8,128)(2,1)}) custom-call(bf16[192,1536]{1,0:T(8,128)(2,1)} %get-tuple-element.373.refs_0_, bf16[192,1536]{1,0:T(8,128)(2,1)} %get-tuple-element.372.refs_1_, bf16[192,1536]{1,0:T(8,128)(2,1)} %collective-permute-done.refs_2_, ...), custom_call_target="tpu_custom_call" | custom-call | flops 3623878656 | bytes 18874368 | tf_op jit(solution)/shard_map/pallas_call | solution.py:298
  93.9 7.0 %fusion.4.placed.refs_0_ = bf16[1536,768]{1,0:T(8,128)(2,1)} fusion(bf16[1536,768]{1,0:T(8,128)(2,1)} %get-tuple-element.195, s32[1536]{0:T(1024)S(1)} %pad_add_fusion, s32[1536]{0:T(1024)S(1)} %reduce.2), kind=kOutput, calls=%fused_computation.4 | convolution fusion | flops 3627417600 | bytes 4730880 | tf_op jit(solution)/shard_map/dot_general | solution.py:24
  101.5 21.3 %shard_map.333 = (bf16[1536,384]{1,0:T(8,128)(2,1)}, bf16[2,1536,1536]{2,1,0:T(8,128)(2,1)}) custom-call(bf16[1536,768]{1,0:T(8,128)(2,1)} %fusion.4.placed.refs_0_, bf16[192,128]{1,0:T(8,128)(2,1)} %bitcast.112, bf16[192,3072]{1,0:T(8,128)(2,1)} %get-tuple-element.196.table), custom_call_target="tpu_custom_call" | custom-call | flops 9663676416 | bytes 14155776 | tf_op jit(solution)/shard_map/pallas_call | solution.py:74
  139.5 8.6 %collective-permute-done.12 = bf16[384,768]{1,0:T(8,128)(2,1)} collective-permute-done((bf16[384,768]{1,0:T(8,128)(2,1)}, bf16[384,768]{1,0:T(8,128)(2,1)}, u32[]{:S(2)}, u32[]{:S(2)}) %collective-permute-start.12) | collective-permute-done | bytes 589856 | tf_op jit(solution)/shard_map/ppermute | solution.py:666
  165.9 31.3 %collective-permute-done.15 = bf16[384,768]{1,0:T(8,128)(2,1)S(1)} collective-permute-done((bf16[384,768]{1,0:T(8,128)(2,1)S(1)}, bf16[384,768]{1,0:T(8,128)(2,1)S(1)}, u32[]{:S(2)}, u32[]{:S(2)}) %collective-permute-start.15) | collective-permute-done | bytes 589856 | tf_op jit(solution)/shard_map/ppermute | solution.py:666
  207.1 28.3 %shard_map.334 = (bf16[384,1536]{1,0:T(8,128)(2,1)}, bf16[384,1536]{1,0:T(8,128)(2,1)}, bf16[384,1536]{1,0:T(8,128)(2,1)}, bf16[384,3072]{1,0:T(8,128)(2,1)}, bf...) custom-call(s32[2]{0:T(128)} %pad_add_fusion.1.refs_0_.where, f32[384,1536]{1,0:T(8,128)} %fusion.17.refs_1_, ...), custom_call_target="tpu_custom_call" | custom-call | flops 14495514624 | bytes 42467328 | tf_op jit(solution)/shard_map/pallas_call | solution.py:404
  235.5 6.6 %shard_map.335 = bf16[4,384,1536]{2,1,0:T(8,128)(2,1)} custom-call(s32[2]{0:T(128)} %pad_add_fusion.1.refs_0_.where, bf16[384,1536]{1,0:T(8,128)(2,1)} %get-tuple-element.213.left, bf16[384,3072]{1,0:T(8,128)(2,1)} %get-tuple-element.214.right), custom_call_target="tpu_custom_call" | custom-call | flops 1811939328 | bytes 11796480 | tf_op jit(solution)/shard_map/pallas_call | solution.py:477
  242.2 6.7 %shard_map.337 = bf16[4,384,1536]{2,1,0:T(8,128)(2,1)} custom-call(s32[2]{0:T(128)} %pad_add_fusion.1.refs_0_.where, bf16[384,3072]{1,0:T(8,128)(2,1)} %get-tuple-element.235.left, bf16[384,1536]{1,0:T(8,128)(2,1)} %bitcast.90), custom_call_target="tpu_custom_call" | custom-call | flops 1811939328 | bytes 14155776 | tf_op jit(solution)/shard_map/pallas_call | solution.py:477
  253.5 8.8 %shard_map.336 = (bf16[384,768]{1,0:T(8,128)(2,1)}, bf16[384,768]{1,0:T(8,128)(2,1)}, bf16[384,768]{1,0:T(8,128)(2,1)}, bf16[384,768]{1,0:T(8,128)(2,1)}, bf16[3...) custom-call(s32[2]{0:T(128)} %pad_add_fusion.1.refs_0_.where, ...), custom_call_target="tpu_custom_call" | custom-call | flops 1811939328 | bytes 11796480 | tf_op jit(solution)/shard_map/pallas_call | solution.py:477
  267.1 10.3 %collective-permute-done.28.refs_6_.refs_3_ = bf16[192,1536]{1,0:T(8,128)(2,1)S(1)} collective-permute-done((bf16[192,1536]{1,0:T(8,128)(2,1)S(1)}, bf16[192,1536]{1,0:T(8,128)(2,1)S(1)}, u32[]{:S(2)}, u32[]{:S(2)}) %collective-permute-start.28) | collective-permute-done | bytes 589856 | tf_op jit(solution)/shard_map/ppermute | solution.py:666
  282.4 8.9 %shard_map.338 = (bf16[384,768]{1,0:T(8,128)(2,1)}, bf16[384,768]{1,0:T(8,128)(2,1)}, bf16[384,768]{1,0:T(8,128)(2,1)}, bf16[384,768]{1,0:T(8,128)(2,1)}, bf16[3...) custom-call(s32[2]{0:T(128)} %pad_add_fusion.1.refs_0_.where, ...), custom_call_target="tpu_custom_call" | custom-call | flops 1811939328 | bytes 14155776 | tf_op jit(solution)/shard_map/pallas_call | solution.py:477
  295.6 9.9 %shard_map.339 = (bf16[1536,384]{1,0:T(8,128)(2,1)}, bf16[192,1536]{1,0:T(8,128)(2,1)}, f32[192,1536]{1,0:T(8,128)}) custom-call(s32[2]{0:T(128)} %pad_add_fusion.1.refs_0_.where, bf16[1536,384]{1,0:T(8,128)(2,1)} %get-tuple-element.200.refs_1_.refs_4_, bf16[384,1536]{1,0:T(8,128)(2,1)} %refs_2_.1, bf16[192,1536]{1,0:T(8,128)(2,1)} %copy-done.8, ...), custom_call_target="tpu_custom_call" | custom-call | flops 3623878656 | bytes 7077888 | tf_op jit(solution)/shard_map/pallas_call | solution.py:517
  312.9 16.5 %shard_map.340 = (bf16[1536,640]{1,0:T(8,128)(2,1)}, f32[192,128]{1,0:T(8,128)}, f32[8,128]{1,0:T(8,128)}) custom-call(bf16[1536,768]{1,0:T(8,128)(2,1)} %fusion.4.placed.refs_0_, bf16[192,128]{1,0:T(8,128)(2,1)} %bitcast.113, bf16[192,3072]{1,0:T(8,128)(2,1)} %get-tuple-element.211.refs_2_, bf16[256,256]{1,0:T(8,128)(2,1)} %fusion.35.refs_3_, ...), custom_call_target="tpu_custom_call" | custom-call | flops 7247757312 | bytes 14155776 | tf_op jit(solution)/shard_map/pallas_call | solution.py:160
  336.0 18.3 %shard_map.341 = (bf16[1536,640]{1,0:T(8,128)(2,1)}, f32[192,128]{1,0:T(8,128)}, f32[8,128]{1,0:T(8,128)}) custom-call(bf16[1536,768]{1,0:T(8,128)(2,1)} %fusion.4.placed.refs_0_, bf16[192,128]{1,0:T(8,128)(2,1)} %bitcast.114, bf16[192,3072]{1,0:T(8,128)(2,1)} %get-tuple-element.211.refs_2_, bf16[256,256]{1,0:T(8,128)(2,1)} %fusion.35.refs_3_, ...), custom_call_target="tpu_custom_call" | custom-call | flops 7247757312 | bytes 14155776 | tf_op jit(solution)/shard_map/pallas_call | solution.py:160
  361.8 18.6 %shard_map.342 = (bf16[1536,640]{1,0:T(8,128)(2,1)}, bf16[384,768]{1,0:T(8,128)(2,1)}, bf16[384,768]{1,0:T(8,128)(2,1)}, bf16[384,768]{1,0:T(8,128)(2,1)}, bf16[...) custom-call(s32[2]{0:T(128)} %pad_add_fusion.1.refs_0_.where, ...), custom_call_target="tpu_custom_call" | custom-call | flops 6039797760 | bytes 13369344 | tf_op jit(solution)/shard_map/pallas_call | solution.py:571
  390.7 8.4 %shard_map.343 = (bf16[4,208,640]{2,1,0:T(8,128)(2,1)}, bf16[4,208,640]{2,1,0:T(8,128)(2,1)}) custom-call(s32[2]{0:T(128)} %pad_add_fusion.1.refs_0_.where, bf16[1536,1536]{1,0:T(8,128)(2,1)} %get-tuple-element.289.hidden, bf16[1536,640]{1,0:T(8,128)(2,1)} %get-tuple-element.290.d_along, f32[8,1536]{1,0:T(8,128)} %get-tuple-element.291.first_sums, ...), custom_call_target="tpu_custom_call" | custom-call | flops 3019898880 | bytes 14548992 | tf_op jit(solution)/shard_map/pallas_call | solution.py:644
  422.0 6.9 %all-to-all-done.1 = bf16[4,208,640]{2,1,0:T(8,128)(2,1)S(1)} async-done(((bf16[4,208,640]{2,1,0:T(8,128)(2,1)}), bf16[4,208,640]{2,1,0:T(8,128)(2,1)S(1)}, u32[]{:S(2)}, u32[]{:S(2)}) %all-to-all-start.1) | async-done | bytes 1064992 | tf_op jit(solution)/shard_map/all_to_all | solution.py:1118
  431.2 10.5 %collective-permute-done.47 = bf16[384,768]{1,0:T(8,128)(2,1)} collective-permute-done((bf16[384,768]{1,0:T(8,128)(2,1)}, bf16[384,768]{1,0:T(8,128)(2,1)}, u32[]{:S(2)}, u32[]{:S(2)}) %collective-permute-start.47) | collective-permute-done | bytes 589856 | tf_op jit(solution)/shard_map/ppermute | solution.py:666
  441.6 11.8 %collective-permute-done.48 = bf16[384,768]{1,0:T(8,128)(2,1)} collective-permute-done((bf16[384,768]{1,0:T(8,128)(2,1)}, bf16[384,768]{1,0:T(8,128)(2,1)}, u32[]{:S(2)}, u32[]{:S(2)}) %collective-permute-start.48) | collective-permute-done | bytes 589856 | tf_op jit(solution)/shard_map/ppermute | solution.py:666
  474.9 12.3 %collective-permute-done.54 = bf16[208,640]{1,0:T(8,128)(2,1)} collective-permute-done((bf16[208,640]{1,0:T(8,128)(2,1)S(1)}, bf16[208,640]{1,0:T(8,128)(2,1)}, u32[]{:S(2)}, u32[]{:S(2)}) %collective-permute-start.54) | collective-permute-done | bytes 266272 | tf_op jit(solution)/shard_map/ppermute | solution.py:833
  490.6 20.1 %collective-permute-done.55 = bf16[208,640]{1,0:T(8,128)(2,1)S(1)} collective-permute-done((bf16[208,640]{1,0:T(8,128)(2,1)S(1)}, bf16[208,640]{1,0:T(8,128)(2,1)S(1)}, u32[]{:S(2)}, u32[]{:S(2)}) %collective-permute-start.55) | collective-permute-done | bytes 266272 | tf_op jit(solution)/shard_map/ppermute | solution.py:833
  510.9 11.1 %collective-permute-done.56 = bf16[416,640]{1,0:T(8,128)(2,1)S(1)} collective-permute-done((bf16[416,640]{1,0:T(8,128)(2,1)S(1)}, bf16[416,640]{1,0:T(8,128)(2,1)S(1)}, u32[]{:S(2)}, u32[]{:S(2)}) %collective-permute-start.56) | collective-permute-done | bytes 532512 | tf_op jit(solution)/shard_map/ppermute | solution.py:833
  (336 shorter events, 206.5 us)
Async XLA Ops:
  40.4 29.8 %all-to-all-start = ((bf16[4,208,640]{2,1,0:T(8,128)(2,1)}), bf16[4,208,640]{2,1,0:T(8,128)(2,1)S(1)}, u32[]{:S(2)}, u32[]{:S(2)}) async-start(bf16[4,208,640]{2,1,0:T(8,128)(2,1)} %fusion.22), calls=%async_computation | async-start | bytes 2129920 | tf_op jit(solution)/shard_map/all_to_all | solution.py:988
  43.9 288.6 %reduce-scatter.4.cloned.1.call-start = ((), (), s32[]{:S(2)}) async-start(), calls=%async_computation.5 | async-start | bytes 737280 | tf_op jit(solution)/shard_map/reduce_scatter | solution.py:1076
  73.7 55.0 %collective-permute-start.7 = (bf16[192,3072]{1,0:T(8,128)(2,1)S(1)}, bf16[192,3072]{1,0:T(8,128)(2,1)}, u32[]{:S(2)}, u32[]{:S(2)}) collective-permute-start(bf16[192,3072]{1,0:T(8,128)(2,1)S(1)} %constant_dynamic-slice_fusion.4), channel_id=1, source_target_pairs={{0,8},{8,0},{16,24},{24,16},{1,9},{9,1},{17,25},{25,17},{2,10},{10... | collective-permute-start | bytes 3538952 | tf_op jit(solution)/shard_map/ppermute | solution.py:666
  75.2 53.5 %collective-permute-start.8 = (bf16[192,3072]{1,0:T(8,128)(2,1)S(1)}, bf16[192,3072]{1,0:T(8,128)(2,1)}, u32[]{:S(2)}, u32[]{:S(2)}) collective-permute-start(bf16[192,3072]{1,0:T(8,128)(2,1)S(1)} %constant_dynamic-slice_fusion.4), channel_id=1, source_target_pairs={{0,16},{8,24},{16,0},{24,8},{1,17},{9,25},{17,1},{25,9},{2,18},{10... | collective-permute-start | bytes 3538952 | tf_op jit(solution)/shard_map/ppermute | solution.py:666
  75.8 52.9 %collective-permute-start.10 = (bf16[384,1536]{1,0:T(8,128)(2,1)S(1)}, bf16[384,1536]{1,0:T(8,128)(2,1)}, u32[]{:S(2)}, u32[]{:S(2)}) collective-permute-start(bf16[384,1536]{1,0:T(8,128)(2,1)S(1)} %copy-done.10), channel_id=1, source_target_pairs={{0,16},{8,24},{16,0},{24,8},{1,17},{9,25},{17,1},{25,9},{2,18},{10... | collective-permute-start | bytes 3538952 | tf_op jit(solution)/shard_map/ppermute | solution.py:666
  77.3 51.4 %collective-permute-start.9 = (bf16[384,1536]{1,0:T(8,128)(2,1)S(1)}, bf16[384,1536]{1,0:T(8,128)(2,1)}, u32[]{:S(2)}, u32[]{:S(2)}) collective-permute-start(bf16[384,1536]{1,0:T(8,128)(2,1)S(1)} %copy-done.10), channel_id=1, source_target_pairs={{0,8},{8,0},{16,24},{24,16},{1,9},{9,1},{17,25},{25,17},{2,10},{10... | collective-permute-start | bytes 3538952 | tf_op jit(solution)/shard_map/ppermute | solution.py:666
  134.5 26.8 %collective-permute-start.13 = (bf16[384,768]{1,0:T(8,128)(2,1)}, bf16[384,768]{1,0:T(8,128)(2,1)}, u32[]{:S(2)}, u32[]{:S(2)}) collective-permute-start(bf16[384,768]{1,0:T(8,128)(2,1)} %slice.130), channel_id=1, source_target_pairs={{0,16},{8,24},{16,0},{24,8},{1,17},{9,25},{17,1},{25,9},{2,18},{10... | collective-permute-start | bytes 1769480 | tf_op jit(solution)/shard_map/ppermute | solution.py:666
  138.9 58.8 %collective-permute-start.19 = (bf16[192,3072]{1,0:T(8,128)(2,1)}, bf16[192,3072]{1,0:T(8,128)(2,1)}, u32[]{:S(2)}, u32[]{:S(2)}) collective-permute-start(bf16[192,3072]{1,0:T(8,128)(2,1)} %collective-permute-done.7.refs_8_), channel_id=1, source_target_pairs={{0,16},{8,24},{16,0},{24,8},{1,17},{9,25},{17,1},{25,9},{2,18},{10... | collective-permute-start | bytes 3538952 | tf_op jit(solution)/shard_map/ppermute | solution.py:666
  148.1 50.1 %collective-permute-start.17 = (bf16[192,3072]{1,0:T(8,128)(2,1)}, bf16[192,3072]{1,0:T(8,128)(2,1)}, u32[]{:S(2)}, u32[]{:S(2)}) collective-permute-start(bf16[192,3072]{1,0:T(8,128)(2,1)} %collective-permute-done.7.refs_8_), channel_id=1, source_target_pairs={{0,1},{1,0},{2,3},{3,2},{4,5},{5,4},{6,7},{7,6},{8,9},{9,8},{10,11... | collective-permute-start | bytes 3538952 | tf_op jit(solution)/shard_map/ppermute | solution.py:887
  148.7 49.1 %collective-permute-start.23 = (bf16[384,1536]{1,0:T(8,128)(2,1)}, bf16[384,1536]{1,0:T(8,128)(2,1)}, u32[]{:S(2)}, u32[]{:S(2)}) collective-permute-start(bf16[384,1536]{1,0:T(8,128)(2,1)} %collective-permute-done.10.refs_17_), channel_id=1, source_target_pairs={{0,8},{8,0},{16,24},{24,16},{1,9},{9,1},{17,25},{25,17},{2,10},{10... | collective-permute-start | bytes 3538952 | tf_op jit(solution)/shard_map/ppermute | solution.py:666
  162.5 34.7 %collective-permute-start.15 = (bf16[384,768]{1,0:T(8,128)(2,1)S(1)}, bf16[384,768]{1,0:T(8,128)(2,1)S(1)}, u32[]{:S(2)}, u32[]{:S(2)}) collective-permute-start(bf16[384,768]{1,0:T(8,128)(2,1)S(1)} %add_convert_fusion.13), channel_id=1, source_target_pairs={{0,16},{8,24},{16,0},{24,8},{1,17},{9,25},{17,1},{25,9},{2,18},{10... | collective-permute-start | bytes 1769480 | tf_op jit(solution)/shard_map/ppermute | solution.py:666
  164.6 32.6 %collective-permute-start.16 = (bf16[384,768]{1,0:T(8,128)(2,1)S(1)}, bf16[384,768]{1,0:T(8,128)(2,1)S(1)}, u32[]{:S(2)}, u32[]{:S(2)}) collective-permute-start(bf16[384,768]{1,0:T(8,128)(2,1)S(1)} %add_convert_fusion.12), channel_id=1, source_target_pairs={{0,8},{8,0},{16,24},{24,16},{1,9},{9,1},{17,25},{25,17},{2,10},{10... | collective-permute-start | bytes 1769480 | tf_op jit(solution)/shard_map/ppermute | solution.py:666
  248.9 31.3 %collective-permute-start.30 = (bf16[4,384,1536]{2,1,0:T(8,128)(2,1)}, bf16[4,384,1536]{2,1,0:T(8,128)(2,1)S(1)}, u32[]{:S(2)}, u32[]{:S(2)}) collective-permute-start(bf16[4,384,1536]{2,1,0:T(8,128)(2,1)} %shard_map.337), channel_id=1, source_target_pairs={{0,1},{1,0},{2,3},{3,2},{4,5},{5,4},{6,7},{7,6},{8,9},{9,8},{10,11... | collective-permute-start | bytes 14155784 | tf_op jit(solution)/shard_map/ppermute | solution.py:887
  309.9 45.3 %all-gather.4.cloned.1.call-start = ((), (), s32[]{:S(2)}) async-start(), calls=%async_computation.6 | async-start | bytes 1327104 | tf_op jit(solution)/shard_map/all_gather | solution.py:1079
  332.6 70.5 %reduce-scatter.6.cloned.1.call-start = ((), (), s32[]{:S(2)}) async-start(), calls=%async_computation.7 | async-start | bytes 1474560 | tf_op jit(solution)/shard_map/reduce_scatter | solution.py:1076
  357.6 107.6 %reduce-scatter.8.cloned.1.call-start = ((), (), s32[]{:S(2)}) async-start(), calls=%async_computation.8 | async-start | bytes 1474560 | tf_op jit(solution)/shard_map/reduce_scatter | solution.py:1076
  359.2 26.6 %collective-permute-start.41 = (bf16[384,768]{1,0:T(8,128)(2,1)S(1)}, bf16[384,768]{1,0:T(8,128)(2,1)S(1)}, u32[]{:S(2)}, u32[]{:S(2)}) collective-permute-start(bf16[384,768]{1,0:T(8,128)(2,1)S(1)} %copy-done.49), channel_id=1, source_target_pairs={{0,8},{8,0},{16,24},{24,16},{1,9},{9,1},{17,25},{25,17},{2,10},{10... | collective-permute-start | bytes 1769480 | tf_op jit(solution)/shard_map/ppermute | solution.py:666
  405.5 116.9 %all-gather.6.cloned.1.call-start = ((), (), s32[]{:S(2)}) async-start(), calls=%async_computation.9 | async-start | bytes 2654208 | tf_op jit(solution)/shard_map/all_gather | solution.py:1079
  413.8 122.8 %all-gather.8.cloned.1.call-start = ((), (), s32[]{:S(2)}) async-start(), calls=%async_computation.10 | async-start | bytes 2654208 | tf_op jit(solution)/shard_map/all_gather | solution.py:1079
  415.0 26.7 %collective-permute-start.47 = (bf16[384,768]{1,0:T(8,128)(2,1)}, bf16[384,768]{1,0:T(8,128)(2,1)}, u32[]{:S(2)}, u32[]{:S(2)}) collective-permute-start(bf16[384,768]{1,0:T(8,128)(2,1)} %get-tuple-element.312), channel_id=1, source_target_pairs={{0,8},{8,0},{16,24},{24,16},{1,9},{9,1},{17,25},{25,17},{2,10},{10... | collective-permute-start | bytes 1769480 | tf_op jit(solution)/shard_map/ppermute | solution.py:666
  416.9 36.6 %collective-permute-start.48 = (bf16[384,768]{1,0:T(8,128)(2,1)}, bf16[384,768]{1,0:T(8,128)(2,1)}, u32[]{:S(2)}, u32[]{:S(2)}) collective-permute-start(bf16[384,768]{1,0:T(8,128)(2,1)} %get-tuple-element.313), channel_id=1, source_target_pairs={{0,8},{8,0},{16,24},{24,16},{1,9},{9,1},{17,25},{25,17},{2,10},{10... | collective-permute-start | bytes 1769480 | tf_op jit(solution)/shard_map/ppermute | solution.py:666
  417.0 36.5 %collective-permute-start.49 = (bf16[384,768]{1,0:T(8,128)(2,1)}, bf16[384,768]{1,0:T(8,128)(2,1)}, u32[]{:S(2)}, u32[]{:S(2)}) collective-permute-start(bf16[384,768]{1,0:T(8,128)(2,1)} %get-tuple-element.314), channel_id=1, source_target_pairs={{0,16},{8,24},{16,0},{24,8},{1,17},{9,25},{17,1},{25,9},{2,18},{10... | collective-permute-start | bytes 1769480 | tf_op jit(solution)/shard_map/ppermute | solution.py:666
  418.9 34.5 %collective-permute-start.50 = (bf16[384,768]{1,0:T(8,128)(2,1)}, bf16[384,768]{1,0:T(8,128)(2,1)}, u32[]{:S(2)}, u32[]{:S(2)}) collective-permute-start(bf16[384,768]{1,0:T(8,128)(2,1)} %get-tuple-element.315), channel_id=1, source_target_pairs={{0,16},{8,24},{16,0},{24,8},{1,17},{9,25},{17,1},{25,9},{2,18},{10... | collective-permute-start | bytes 1769480 | tf_op jit(solution)/shard_map/ppermute | solution.py:666
  429.7 35.5 %collective-permute-start.53 = (bf16[416,640]{1,0:T(8,128)(2,1)}, bf16[416,640]{1,0:T(8,128)(2,1)}, u32[]{:S(2)}, u32[]{:S(2)}) collective-permute-start(bf16[416,640]{1,0:T(8,128)(2,1)} %constant_dynamic-slice_fusion.2), channel_id=1, source_target_pairs={{0,2},{2,0},{4,6},{6,4},{1,3},{3,1},{5,7},{7,5},{8,10},{10,8},{12,... | collective-permute-start | bytes 1597448 | tf_op jit(solution)/shard_map/ppermute | solution.py:833
  (94 other events, 1316.0 us)
Sparse Core Ops, SparseCore 0:
  310.0 22.4 reduce-scatter.3
  334.1 21.0 all-gather.3
  358.1 28.9 reduce-scatter.5
  405.6 28.2 reduce-scatter.7
  435.3 31.3 all-gather.5
  468.7 43.3 all-gather.7

commit v2 on v1

--- a/solution.py
+++ b/solution.py
@@ -764,8 +764,8 @@
     pin_all(exchanges, array)
 
 
-def pin_some(exchanges, *arrays):
-    firsts = [max(e.new) for e in exchanges]
+def pin_some(exchanges, *arrays, firsts=None):
+    firsts = firsts or [max(e.new) for e in exchanges]
     out = pin(*arrays, *[e.new[k] for e, k in zip(exchanges, firsts)])
     for e, k, block in zip(exchanges, firsts, out[len(arrays) :]):
         e.new[k] = block
@@ -1042,6 +1042,7 @@
         g.send()
     came_inner = other_core(half_gradient(seq_count, True, where, hidden_two, d_inner))
     outer_away = half_gradient(seq_count, False, where, activated, grad_rows)
+    (outer_away,) = pin_some(d_mixed_gathers, outer_away, firsts=[up[0], down[0]])
     came_outer = other_core(outer_away)
     kept_inner = half_gradient(seq_count, True, where, hidden_two, d_inner, came_inner)
     kept_inner = pin_all(d_mixed_gathers, *kept_inner)
@@ -1097,8 +1098,9 @@
     d_along, *d_normed, first_sums = rows_back(
         seq_count, where, order[None], d_heads, window, weight_whole
     )
-    out = pin_all(outer_sums_of, d_along, *d_normed)
-    d_along, d_normed = out[0], out[1:]
+    out = pin_all(outer_sums_of, d_along, inner_sum, *d_normed)
+    d_along, inner_sum, d_normed = out[0], out[1], out[2:]
+    inner_sum = gather_windows(inner_sum)
     for step in range(1, len(up)):
         send_all(outer_sums_of)
     arrived = [
@@ -1108,10 +1110,9 @@
     results = pack(
         seq_count, where, hidden_one, d_along, first_sums, sums, inner_sums, d_bias, d_rel
     )
-    *results, inner_sum = pin_all(outer_sums_of, *results, inner_sum)
+    results = pin_all(outer_sums_of, *results)
     packed_core = OtherCore(results[1])
     outer_sum = scatter_windows(joined_sum(outer_sums_of))
-    inner_sum = gather_windows(inner_sum)
     (packed,) = pin_all([packed_core], results[0])
     packed = (packed.astype(F32) + packed_core.new[0].astype(F32)).astype(BF16)
     packed_shape = packed.shape
@@ -1120,17 +1121,18 @@
     take_after(arrived, packed)
     packed_cube = CubeSum(packed.reshape(-1, packed_shape[2]), wz_count)
     packed_cube.send()
-    (outer_sum,) = pin_all([packed_cube], outer_sum)
+    take_after(arrived, packed_cube.new[0])
+    packed_cube.send()
+    (outer_sum,) = pin_all(arrived, outer_sum)
     outer_sum = gather_windows(outer_sum)
-    packed_cube.send()
-    d_mixed_blocks = pin_all(arrived, *d_mixed_blocks)
     for step in range(1, len(up)):
         send_all(arrived)
+    take_after(arrived, packed_cube.new[0])
+    d_mixed_blocks = pin(packed_cube.new[0], *d_mixed_blocks)[1:]
+    packed_cube.send()
     returned = returned_rows(
         seq_count, where, order.reshape(2 * seq_count, row_count // 2), d_mixed_blocks
     )
-    (returned,) = pin_all([packed_cube], returned)
-    packed_cube.send()
     own_unit, own_scale = norm_of(inputs[0].astype(F32))
     arrived = jnp.concatenate([g.rest() for g in arrived], axis=1)
     grad_inputs = norm_back(own_unit, own_scale, vectors[0:1], arrived) + returned
@@ -1140,7 +1142,7 @@
         return jnp.concatenate([pieces[:half], pieces[half:]], axis=axis).astype(F32)
 
     grad_out_w = both_halves(out_sum, 0)
-    grad_inputs, grad_out_w = pin_all([packed_cube], grad_inputs, grad_out_w)
+    (grad_inputs,) = pin_all([packed_cube], grad_inputs)
     packed_cube.send()
     grad_inner_w = both_halves(inner_sum, 1)
     grad_outer_w = both_halves(outer_sum, 0)

time: 558 us -> 559 us (level)
    unnamed x109 -> x103, local copies, waits for them, and re-layouts: 8.41 us -> 11.2 us
  transfers between devices with their start and end apart: 66 -> 66, of which waited for: 36 -> 33; matrix products, arithmetic and copies ran while one was open for 12% -> 11% of each run, Pallas kernels for 26% -> 26%
where the time goes in v2:
time: 559 us; the launch traced here: 549 us
  waiting for transfers between devices  206 us (37%)
  Pallas kernels  178 us (32%)
  starting transfers between devices  61.7 us (11%)
  other arithmetic  41.1 us (7%)
  local copies, waits for them, and re-layouts  29.3 us (5%)
  matrix products  17.8 us (3%)
  between operations  15.5 us (3%)
    ppermute x42, waiting for transfers between devices, swap(): return lax.ppermute(array, 'seq', [(i, i ^ mask) for i in range(count)])  144 us
    ppermute x42, starting transfers between devices, swap(): return lax.ppermute(array, 'seq', [(i, i ^ mask) for i in range(count)])  46.7 us
    ppermute x4, waiting for transfers between devices, swap(): return lax.ppermute(array, 'wz', [(i, i ^ bit) for i in range(self.count)])  41.8 us
    pallas_call x2, Pallas kernels, attend_back(): pl.pallas_call(functools.partial(attend_back_kernel, heads, head, rows),...  34.8 us
    pallas_call x4, Pallas kernels, half_gradient(): pl.pallas_call(functools.partial(half_kernel, count, split, away), grid=(...  30.9 us
    pallas_call x1, Pallas kernels, feed_forward(): pl.pallas_call(functools.partial(feed_kernel, count, chunk), in_specs=[sc...  28.4 us
    pallas_call x1, Pallas kernels, attend(): pl.pallas_call(functools.partial(attend_kernel, heads, rows), grid=(lengt...  21.3 us
    pallas_call x1, Pallas kernels, rows_back(): pl.pallas_call(functools.partial(rows_back_kernel, count), grid=(count,),...  18.6 us
  transfers between devices with their start and end apart: 66, of which 33 were waited for; matrix products, arithmetic and copies ran while one was open for 11% of the time, Pallas kernels for 26%

profile of v2, /device:TPU:0, one launch (start us, length us, event | category | flops | bytes accessed | tf_op | source)
XLA Modules:
  0.0 548.9 jit_solution(1567099388798265359)
XLA Ops:
  29.2 9.7 %collective-permute-done.2.refs_3_ = bf16[192,1536]{1,0:T(8,128)(2,1)} collective-permute-done((bf16[192,1536]{1,0:T(8,128)(2,1)}, bf16[192,1536]{1,0:T(8,128)(2,1)}, u32[]{:S(2)}, u32[]{:S(2)}) %collective-permute-start.2) | collective-permute-done | bytes 589856 | tf_op jit(solution)/shard_map/ppermute | solution.py:666
  47.4 22.0 %collective-permute-done.4.refs_6_ = bf16[192,1536]{1,0:T(8,128)(2,1)S(1)} collective-permute-done((bf16[192,1536]{1,0:T(8,128)(2,1)}, bf16[192,1536]{1,0:T(8,128)(2,1)S(1)}, u32[]{:S(2)}, u32[]{:S(2)}) %collective-permute-start.4) | collective-permute-done | bytes 589856 | tf_op jit(solution)/shard_map/ppermute | solution.py:666
  81.4 12.4 %shard_map.331 = (bf16[1536,1536]{1,0:T(8,128)(2,1)}, bf16[1536,1536]{1,0:T(8,128)(2,1)}, bf16[1536,768]{1,0:T(8,128)(2,1)}, bf16[1536,640]{1,0:T(8,128)(2,1)}) custom-call(bf16[192,1536]{1,0:T(8,128)(2,1)} %get-tuple-element.383.refs_0_, bf16[192,1536]{1,0:T(8,128)(2,1)} %get-tuple-element.382.refs_1_, bf16[192,1536]{1,0:T(8,128)(2,1)} %collective-permute-done.refs_2_, ...), custom_call_target="tpu_custom_call" | custom-call | flops 3623878656 | bytes 18874368 | tf_op jit(solution)/shard_map/pallas_call | solution.py:298
  93.9 7.0 %fusion.4.placed.refs_0_ = bf16[1536,768]{1,0:T(8,128)(2,1)} fusion(bf16[1536,768]{1,0:T(8,128)(2,1)} %get-tuple-element.200, s32[1536]{0:T(1024)S(1)} %pad_add_fusion, s32[1536]{0:T(1024)S(1)} %reduce.2), kind=kOutput, calls=%fused_computation.4 | convolution fusion | flops 3627417600 | bytes 4730880 | tf_op jit(solution)/shard_map/dot_general | solution.py:24
  101.5 21.3 %shard_map.333 = (bf16[1536,384]{1,0:T(8,128)(2,1)}, bf16[2,1536,1536]{2,1,0:T(8,128)(2,1)}) custom-call(bf16[1536,768]{1,0:T(8,128)(2,1)} %fusion.4.placed.refs_0_, bf16[192,128]{1,0:T(8,128)(2,1)} %bitcast.112, bf16[192,3072]{1,0:T(8,128)(2,1)} %get-tuple-element.201.table), custom_call_target="tpu_custom_call" | custom-call | flops 9663676416 | bytes 14155776 | tf_op jit(solution)/shard_map/pallas_call | solution.py:74
  139.5 8.6 %collective-permute-done.12 = bf16[384,768]{1,0:T(8,128)(2,1)} collective-permute-done((bf16[384,768]{1,0:T(8,128)(2,1)}, bf16[384,768]{1,0:T(8,128)(2,1)}, u32[]{:S(2)}, u32[]{:S(2)}) %collective-permute-start.12) | collective-permute-done | bytes 589856 | tf_op jit(solution)/shard_map/ppermute | solution.py:666
  165.9 31.3 %collective-permute-done.15 = bf16[384,768]{1,0:T(8,128)(2,1)S(1)} collective-permute-done((bf16[384,768]{1,0:T(8,128)(2,1)S(1)}, bf16[384,768]{1,0:T(8,128)(2,1)S(1)}, u32[]{:S(2)}, u32[]{:S(2)}) %collective-permute-start.15) | collective-permute-done | bytes 589856 | tf_op jit(solution)/shard_map/ppermute | solution.py:666
  207.2 28.4 %shard_map.334 = (bf16[384,1536]{1,0:T(8,128)(2,1)}, bf16[384,1536]{1,0:T(8,128)(2,1)}, bf16[384,1536]{1,0:T(8,128)(2,1)}, bf16[384,3072]{1,0:T(8,128)(2,1)}, bf...) custom-call(s32[2]{0:T(128)} %pad_add_fusion.1.refs_0_.where, f32[384,1536]{1,0:T(8,128)} %fusion.17.refs_1_, ...), custom_call_target="tpu_custom_call" | custom-call | flops 14495514624 | bytes 42467328 | tf_op jit(solution)/shard_map/pallas_call | solution.py:404
  235.5 6.7 %shard_map.335 = bf16[4,384,1536]{2,1,0:T(8,128)(2,1)} custom-call(s32[2]{0:T(128)} %pad_add_fusion.1.refs_0_.where, bf16[384,1536]{1,0:T(8,128)(2,1)} %get-tuple-element.218.left, bf16[384,3072]{1,0:T(8,128)(2,1)} %get-tuple-element.219.right), custom_call_target="tpu_custom_call" | custom-call | flops 1811939328 | bytes 11796480 | tf_op jit(solution)/shard_map/pallas_call | solution.py:477
  244.6 6.5 %shard_map.337 = bf16[4,384,1536]{2,1,0:T(8,128)(2,1)} custom-call(s32[2]{0:T(128)} %pad_add_fusion.1.refs_0_.where, bf16[384,3072]{1,0:T(8,128)(2,1)} %get-tuple-element.228.left, bf16[384,1536]{1,0:T(8,128)(2,1)} %bitcast.90), custom_call_target="tpu_custom_call" | custom-call | flops 1811939328 | bytes 14155776 | tf_op jit(solution)/shard_map/pallas_call | solution.py:477
  251.1 7.0 %collective-permute-done.26.refs_5_.refs_2_ = bf16[192,1536]{1,0:T(8,128)(2,1)S(1)} collective-permute-done((bf16[192,1536]{1,0:T(8,128)(2,1)S(1)}, bf16[192,1536]{1,0:T(8,128)(2,1)S(1)}, u32[]{:S(2)}, u32[]{:S(2)}) %collective-permute-start.26) | collective-permute-done | bytes 589856 | tf_op jit(solution)/shard_map/ppermute | solution.py:666
  260.8 8.8 %shard_map.336 = (bf16[384,768]{1,0:T(8,128)(2,1)}, bf16[384,768]{1,0:T(8,128)(2,1)}, bf16[384,768]{1,0:T(8,128)(2,1)}, bf16[384,768]{1,0:T(8,128)(2,1)}, bf16[3...) custom-call(s32[2]{0:T(128)} %pad_add_fusion.1.refs_0_.where, ...), custom_call_target="tpu_custom_call" | custom-call | flops 1811939328 | bytes 11796480 | tf_op jit(solution)/shard_map/pallas_call | solution.py:477
  279.7 8.9 %shard_map.338 = (bf16[384,768]{1,0:T(8,128)(2,1)}, bf16[384,768]{1,0:T(8,128)(2,1)}, bf16[384,768]{1,0:T(8,128)(2,1)}, bf16[384,768]{1,0:T(8,128)(2,1)}, bf16[3...) custom-call(s32[2]{0:T(128)} %pad_add_fusion.1.refs_0_.where, ...), custom_call_target="tpu_custom_call" | custom-call | flops 1811939328 | bytes 14155776 | tf_op jit(solution)/shard_map/pallas_call | solution.py:477
  292.6 9.9 %shard_map.339 = (bf16[1536,384]{1,0:T(8,128)(2,1)}, bf16[192,1536]{1,0:T(8,128)(2,1)}, f32[192,1536]{1,0:T(8,128)}) custom-call(s32[2]{0:T(128)} %pad_add_fusion.1.refs_0_.where, bf16[1536,384]{1,0:T(8,128)(2,1)} %get-tuple-element.205.refs_1_.refs_4_, bf16[384,1536]{1,0:T(8,128)(2,1)} %refs_2_.1, bf16[192,1536]{1,0:T(8,128)(2,1)} %copy-done.8, ...), custom_call_target="tpu_custom_call" | custom-call | flops 3623878656 | bytes 7077888 | tf_op jit(solution)/shard_map/pallas_call | solution.py:517
  310.4 16.5 %shard_map.340 = (bf16[1536,640]{1,0:T(8,128)(2,1)}, f32[192,128]{1,0:T(8,128)}, f32[8,128]{1,0:T(8,128)}) custom-call(bf16[1536,768]{1,0:T(8,128)(2,1)} %fusion.4.placed.refs_0_, bf16[192,128]{1,0:T(8,128)(2,1)} %bitcast.113, bf16[192,3072]{1,0:T(8,128)(2,1)} %get-tuple-element.216.refs_2_, bf16[256,256]{1,0:T(8,128)(2,1)} %fusion.35.refs_3_, ...), custom_call_target="tpu_custom_call" | custom-call | flops 7247757312 | bytes 14155776 | tf_op jit(solution)/shard_map/pallas_call | solution.py:160
  333.5 18.3 %shard_map.341 = (bf16[1536,640]{1,0:T(8,128)(2,1)}, f32[192,128]{1,0:T(8,128)}, f32[8,128]{1,0:T(8,128)}) custom-call(bf16[1536,768]{1,0:T(8,128)(2,1)} %fusion.4.placed.refs_0_, bf16[192,128]{1,0:T(8,128)(2,1)} %bitcast.114, bf16[192,3072]{1,0:T(8,128)(2,1)} %get-tuple-element.216.refs_2_, bf16[256,256]{1,0:T(8,128)(2,1)} %fusion.35.refs_3_, ...), custom_call_target="tpu_custom_call" | custom-call | flops 7247757312 | bytes 14155776 | tf_op jit(solution)/shard_map/pallas_call | solution.py:160
  359.3 18.6 %shard_map.342 = (bf16[1536,640]{1,0:T(8,128)(2,1)}, bf16[384,768]{1,0:T(8,128)(2,1)}, bf16[384,768]{1,0:T(8,128)(2,1)}, bf16[384,768]{1,0:T(8,128)(2,1)}, bf16[...) custom-call(s32[2]{0:T(128)} %pad_add_fusion.1.refs_0_.where, ...), custom_call_target="tpu_custom_call" | custom-call | flops 6039797760 | bytes 13369344 | tf_op jit(solution)/shard_map/pallas_call | solution.py:571
  388.4 8.4 %shard_map.343 = (bf16[4,208,640]{2,1,0:T(8,128)(2,1)}, bf16[4,208,640]{2,1,0:T(8,128)(2,1)}) custom-call(s32[2]{0:T(128)} %pad_add_fusion.1.refs_0_.where, bf16[1536,1536]{1,0:T(8,128)(2,1)} %get-tuple-element.305.hidden, bf16[1536,640]{1,0:T(8,128)(2,1)} %get-tuple-element.306.d_along, f32[8,1536]{1,0:T(8,128)} %get-tuple-element.307.first_sums, ...), custom_call_target="tpu_custom_call" | custom-call | flops 3019898880 | bytes 14548992 | tf_op jit(solution)/shard_map/pallas_call | solution.py:644
  416.1 10.7 %all-to-all-done.1 = bf16[4,208,640]{2,1,0:T(8,128)(2,1)S(1)} async-done(((bf16[4,208,640]{2,1,0:T(8,128)(2,1)}), bf16[4,208,640]{2,1,0:T(8,128)(2,1)S(1)}, u32[]{:S(2)}, u32[]{:S(2)}) %all-to-all-start.1) | async-done | bytes 1064992 | tf_op jit(solution)/shard_map/all_to_all | solution.py:1119
  428.7 10.8 %collective-permute-done.48 = bf16[384,768]{1,0:T(8,128)(2,1)} collective-permute-done((bf16[384,768]{1,0:T(8,128)(2,1)}, bf16[384,768]{1,0:T(8,128)(2,1)}, u32[]{:S(2)}, u32[]{:S(2)}) %collective-permute-start.48) | collective-permute-done | bytes 589856 | tf_op jit(solution)/shard_map/ppermute | solution.py:666
  439.5 11.8 %collective-permute-done.49 = bf16[384,768]{1,0:T(8,128)(2,1)} collective-permute-done((bf16[384,768]{1,0:T(8,128)(2,1)}, bf16[384,768]{1,0:T(8,128)(2,1)}, u32[]{:S(2)}, u32[]{:S(2)}) %collective-permute-start.49) | collective-permute-done | bytes 589856 | tf_op jit(solution)/shard_map/ppermute | solution.py:666
  460.2 14.9 %collective-permute-done.52 = bf16[208,640]{1,0:T(8,128)(2,1)} collective-permute-done((bf16[208,640]{1,0:T(8,128)(2,1)S(1)}, bf16[208,640]{1,0:T(8,128)(2,1)}, u32[]{:S(2)}, u32[]{:S(2)}) %collective-permute-start.52) | collective-permute-done | bytes 266272 | tf_op jit(solution)/shard_map/ppermute | solution.py:833
  476.2 6.4 %shard_map.344 = f32[384,1536]{1,0:T(8,128)} custom-call(s32[2]{0:T(128)} %pad_add_fusion.1.refs_0_.where, s32[8,192]{1,0:T(8,128)} %reshape_squeeze.3.order, bf16[192,1536]{1,0:T(8,128)(2,1)} %copy-done.8, bf16[192,1536]{1,0:T(8,128)(2,1)} %copy-done.7, bf16[192,1536]{1,0:T(8,128)(2,1)} %copy-done.23, ...), custom_call_target="tpu_custom_call" | custom-call | flops 1811939328 | bytes 7077888 | tf_op jit(solution)/shard_map/pallas_call | solution.py:697
  498.8 21.0 %collective-permute-done.56 = bf16[416,640]{1,0:T(8,128)(2,1)S(1)} collective-permute-done((bf16[416,640]{1,0:T(8,128)(2,1)S(1)}, bf16[416,640]{1,0:T(8,128)(2,1)S(1)}, u32[]{:S(2)}, u32[]{:S(2)}) %collective-permute-start.56) | collective-permute-done | bytes 532512 | tf_op jit(solution)/shard_map/ppermute | solution.py:833
  (330 shorter events, 207.4 us)
Async XLA Ops:
  40.4 29.8 %all-to-all-start = ((bf16[4,208,640]{2,1,0:T(8,128)(2,1)}), bf16[4,208,640]{2,1,0:T(8,128)(2,1)S(1)}, u32[]{:S(2)}, u32[]{:S(2)}) async-start(bf16[4,208,640]{2,1,0:T(8,128)(2,1)} %fusion.22), calls=%async_computation | async-start | bytes 2129920 | tf_op jit(solution)/shard_map/all_to_all | solution.py:988
  43.9 286.1 %reduce-scatter.4.cloned.1.call-start = ((), (), s32[]{:S(2)}) async-start(), calls=%async_computation.5 | async-start | bytes 737280 | tf_op jit(solution)/shard_map/reduce_scatter | solution.py:1077
  73.7 55.0 %collective-permute-start.7 = (bf16[192,3072]{1,0:T(8,128)(2,1)S(1)}, bf16[192,3072]{1,0:T(8,128)(2,1)}, u32[]{:S(2)}, u32[]{:S(2)}) collective-permute-start(bf16[192,3072]{1,0:T(8,128)(2,1)S(1)} %constant_dynamic-slice_fusion.4), channel_id=1, source_target_pairs={{0,8},{8,0},{16,24},{24,16},{1,9},{9,1},{17,25},{25,17},{2,10},{10... | collective-permute-start | bytes 3538952 | tf_op jit(solution)/shard_map/ppermute | solution.py:666
  75.3 53.5 %collective-permute-start.8 = (bf16[192,3072]{1,0:T(8,128)(2,1)S(1)}, bf16[192,3072]{1,0:T(8,128)(2,1)}, u32[]{:S(2)}, u32[]{:S(2)}) collective-permute-start(bf16[192,3072]{1,0:T(8,128)(2,1)S(1)} %constant_dynamic-slice_fusion.4), channel_id=1, source_target_pairs={{0,16},{8,24},{16,0},{24,8},{1,17},{9,25},{17,1},{25,9},{2,18},{10... | collective-permute-start | bytes 3538952 | tf_op jit(solution)/shard_map/ppermute | solution.py:666
  75.8 52.9 %collective-permute-start.10 = (bf16[384,1536]{1,0:T(8,128)(2,1)S(1)}, bf16[384,1536]{1,0:T(8,128)(2,1)}, u32[]{:S(2)}, u32[]{:S(2)}) collective-permute-start(bf16[384,1536]{1,0:T(8,128)(2,1)S(1)} %copy-done.10), channel_id=1, source_target_pairs={{0,16},{8,24},{16,0},{24,8},{1,17},{9,25},{17,1},{25,9},{2,18},{10... | collective-permute-start | bytes 3538952 | tf_op jit(solution)/shard_map/ppermute | solution.py:666
  77.3 51.4 %collective-permute-start.9 = (bf16[384,1536]{1,0:T(8,128)(2,1)S(1)}, bf16[384,1536]{1,0:T(8,128)(2,1)}, u32[]{:S(2)}, u32[]{:S(2)}) collective-permute-start(bf16[384,1536]{1,0:T(8,128)(2,1)S(1)} %copy-done.10), channel_id=1, source_target_pairs={{0,8},{8,0},{16,24},{24,16},{1,9},{9,1},{17,25},{25,17},{2,10},{10... | collective-permute-start | bytes 3538952 | tf_op jit(solution)/shard_map/ppermute | solution.py:666
  134.6 26.8 %collective-permute-start.13 = (bf16[384,768]{1,0:T(8,128)(2,1)}, bf16[384,768]{1,0:T(8,128)(2,1)}, u32[]{:S(2)}, u32[]{:S(2)}) collective-permute-start(bf16[384,768]{1,0:T(8,128)(2,1)} %slice.130), channel_id=1, source_target_pairs={{0,16},{8,24},{16,0},{24,8},{1,17},{9,25},{17,1},{25,9},{2,18},{10... | collective-permute-start | bytes 1769480 | tf_op jit(solution)/shard_map/ppermute | solution.py:666
  138.9 58.8 %collective-permute-start.19 = (bf16[192,3072]{1,0:T(8,128)(2,1)}, bf16[192,3072]{1,0:T(8,128)(2,1)}, u32[]{:S(2)}, u32[]{:S(2)}) collective-permute-start(bf16[192,3072]{1,0:T(8,128)(2,1)} %collective-permute-done.7.refs_8_), channel_id=1, source_target_pairs={{0,16},{8,24},{16,0},{24,8},{1,17},{9,25},{17,1},{25,9},{2,18},{10... | collective-permute-start | bytes 3538952 | tf_op jit(solution)/shard_map/ppermute | solution.py:666
  148.2 50.1 %collective-permute-start.17 = (bf16[192,3072]{1,0:T(8,128)(2,1)}, bf16[192,3072]{1,0:T(8,128)(2,1)}, u32[]{:S(2)}, u32[]{:S(2)}) collective-permute-start(bf16[192,3072]{1,0:T(8,128)(2,1)} %collective-permute-done.7.refs_8_), channel_id=1, source_target_pairs={{0,1},{1,0},{2,3},{3,2},{4,5},{5,4},{6,7},{7,6},{8,9},{9,8},{10,11... | collective-permute-start | bytes 3538952 | tf_op jit(solution)/shard_map/ppermute | solution.py:887
  148.7 49.1 %collective-permute-start.23 = (bf16[384,1536]{1,0:T(8,128)(2,1)}, bf16[384,1536]{1,0:T(8,128)(2,1)}, u32[]{:S(2)}, u32[]{:S(2)}) collective-permute-start(bf16[384,1536]{1,0:T(8,128)(2,1)} %collective-permute-done.10.refs_17_), channel_id=1, source_target_pairs={{0,8},{8,0},{16,24},{24,16},{1,9},{9,1},{17,25},{25,17},{2,10},{10... | collective-permute-start | bytes 3538952 | tf_op jit(solution)/shard_map/ppermute | solution.py:666
  162.6 34.7 %collective-permute-start.15 = (bf16[384,768]{1,0:T(8,128)(2,1)S(1)}, bf16[384,768]{1,0:T(8,128)(2,1)S(1)}, u32[]{:S(2)}, u32[]{:S(2)}) collective-permute-start(bf16[384,768]{1,0:T(8,128)(2,1)S(1)} %add_convert_fusion.13), channel_id=1, source_target_pairs={{0,16},{8,24},{16,0},{24,8},{1,17},{9,25},{17,1},{25,9},{2,18},{10... | collective-permute-start | bytes 1769480 | tf_op jit(solution)/shard_map/ppermute | solution.py:666
  164.6 32.6 %collective-permute-start.16 = (bf16[384,768]{1,0:T(8,128)(2,1)S(1)}, bf16[384,768]{1,0:T(8,128)(2,1)S(1)}, u32[]{:S(2)}, u32[]{:S(2)}) collective-permute-start(bf16[384,768]{1,0:T(8,128)(2,1)S(1)} %add_convert_fusion.12), channel_id=1, source_target_pairs={{0,8},{8,0},{16,24},{24,16},{1,9},{9,1},{17,25},{25,17},{2,10},{10... | collective-permute-start | bytes 1769480 | tf_op jit(solution)/shard_map/ppermute | solution.py:666
  307.3 45.4 %all-gather.4.cloned.1.call-start = ((), (), s32[]{:S(2)}) async-start(), calls=%async_computation.6 | async-start | bytes 1327104 | tf_op jit(solution)/shard_map/all_gather | solution.py:1080
  330.0 55.0 %reduce-scatter.6.cloned.1.call-start = ((), (), s32[]{:S(2)}) async-start(), calls=%async_computation.7 | async-start | bytes 1474560 | tf_op jit(solution)/shard_map/reduce_scatter | solution.py:1077
  355.1 98.2 %reduce-scatter.8.cloned.1.call-start = ((), (), s32[]{:S(2)}) async-start(), calls=%async_computation.8 | async-start | bytes 1474560 | tf_op jit(solution)/shard_map/reduce_scatter | solution.py:1077
  356.7 26.8 %collective-permute-start.41 = (bf16[384,768]{1,0:T(8,128)(2,1)}, bf16[384,768]{1,0:T(8,128)(2,1)S(1)}, u32[]{:S(2)}, u32[]{:S(2)}) collective-permute-start(bf16[384,768]{1,0:T(8,128)(2,1)} %get-tuple-element.299), channel_id=1, source_target_pairs={{0,8},{8,0},{16,24},{24,16},{1,9},{9,1},{17,25},{25,17},{2,10},{10... | collective-permute-start | bytes 1769480 | tf_op jit(solution)/shard_map/ppermute | solution.py:666
  357.3 26.3 %collective-permute-start.42 = (bf16[384,768]{1,0:T(8,128)(2,1)}, bf16[384,768]{1,0:T(8,128)(2,1)S(1)}, u32[]{:S(2)}, u32[]{:S(2)}) collective-permute-start(bf16[384,768]{1,0:T(8,128)(2,1)} %get-tuple-element.300), channel_id=1, source_target_pairs={{0,16},{8,24},{16,0},{24,8},{1,17},{9,25},{17,1},{25,9},{2,18},{10... | collective-permute-start | bytes 1769480 | tf_op jit(solution)/shard_map/ppermute | solution.py:666
  403.5 119.8 %all-gather.6.cloned.1.call-start = ((), (), s32[]{:S(2)}) async-start(), calls=%async_computation.9 | async-start | bytes 2654208 | tf_op jit(solution)/shard_map/all_gather | solution.py:1080
  411.6 125.5 %all-gather.8.cloned.1.call-start = ((), (), s32[]{:S(2)}) async-start(), calls=%async_computation.10 | async-start | bytes 2654208 | tf_op jit(solution)/shard_map/all_gather | solution.py:1080
  411.9 27.6 %collective-permute-start.48 = (bf16[384,768]{1,0:T(8,128)(2,1)}, bf16[384,768]{1,0:T(8,128)(2,1)}, u32[]{:S(2)}, u32[]{:S(2)}) collective-permute-start(bf16[384,768]{1,0:T(8,128)(2,1)} %get-tuple-element.326), channel_id=1, source_target_pairs={{0,8},{8,0},{16,24},{24,16},{1,9},{9,1},{17,25},{25,17},{2,10},{10... | collective-permute-start | bytes 1769480 | tf_op jit(solution)/shard_map/ppermute | solution.py:666
  413.9 37.4 %collective-permute-start.49 = (bf16[384,768]{1,0:T(8,128)(2,1)}, bf16[384,768]{1,0:T(8,128)(2,1)}, u32[]{:S(2)}, u32[]{:S(2)}) collective-permute-start(bf16[384,768]{1,0:T(8,128)(2,1)} %get-tuple-element.327), channel_id=1, source_target_pairs={{0,8},{8,0},{16,24},{24,16},{1,9},{9,1},{17,25},{25,17},{2,10},{10... | collective-permute-start | bytes 1769480 | tf_op jit(solution)/shard_map/ppermute | solution.py:666
  414.0 37.3 %collective-permute-start.50 = (bf16[384,768]{1,0:T(8,128)(2,1)}, bf16[384,768]{1,0:T(8,128)(2,1)}, u32[]{:S(2)}, u32[]{:S(2)}) collective-permute-start(bf16[384,768]{1,0:T(8,128)(2,1)} %get-tuple-element.328), channel_id=1, source_target_pairs={{0,16},{8,24},{16,0},{24,8},{1,17},{9,25},{17,1},{25,9},{2,18},{10... | collective-permute-start | bytes 1769480 | tf_op jit(solution)/shard_map/ppermute | solution.py:666
  416.0 35.4 %collective-permute-start.51 = (bf16[384,768]{1,0:T(8,128)(2,1)}, bf16[384,768]{1,0:T(8,128)(2,1)}, u32[]{:S(2)}, u32[]{:S(2)}) collective-permute-start(bf16[384,768]{1,0:T(8,128)(2,1)} %get-tuple-element.329), channel_id=1, source_target_pairs={{0,16},{8,24},{16,0},{24,8},{1,17},{9,25},{17,1},{25,9},{2,18},{10... | collective-permute-start | bytes 1769480 | tf_op jit(solution)/shard_map/ppermute | solution.py:666
  455.3 27.3 %collective-permute-start.54 = (bf16[384,768]{1,0:T(8,128)(2,1)}, bf16[384,768]{1,0:T(8,128)(2,1)}, u32[]{:S(2)}, u32[]{:S(2)}) collective-permute-start(bf16[384,768]{1,0:T(8,128)(2,1)} %add_convert_fusion.1), channel_id=1, source_target_pairs={{0,8},{8,0},{16,24},{24,16},{1,9},{9,1},{17,25},{25,17},{2,10},{10... | collective-permute-start | bytes 1769480 | tf_op jit(solution)/shard_map/ppermute | solution.py:666
  (91 other events, 1288.9 us)
Sparse Core Ops, SparseCore 0:
  307.4 22.5 reduce-scatter.3
  331.6 21.0 all-gather.3
  355.6 28.9 reduce-scatter.5
  403.6 28.0 reduce-scatter.7
  433.2 42.0 all-gather.5
  476.8 37.1 all-gather.7
